TPU v7x, 32 devices: a whole 2x2x4 slice. The times are simulated.
32 devices in a mesh: parts: 2 (over y), tm: 4 (over z), dp: 4 (over x, core).
Axes of the slice: x: 2, y: 2, z: 4, core: 2. Of those that a mesh axis runs over, the one named last changes fastest.
Arguments:
- signal: bfloat16 [16, 512, 2048], P(('parts', 'dp'), 'tm'), parts along dimension 0, may hold values from -112 to 112
- weight: float32 [640, 2048], P('parts', 'tm'), parts along dimension 0, may hold values from -0.3125 to 0.3125
- first_moment: float32 [640, 2048], P('parts', 'tm'), parts along dimension 0, may hold values from -0.625 to 0.625
- second_moment: float32 [640, 2048], P('parts', 'tm'), parts along dimension 0, may hold values from 0.001 to 0.01
- shuffle: int32 [2048], replicated, may hold values from 0 to 2047, each once
Outputs:
- reconstruction: bfloat16 [16, 512, 2048], P(('parts', 'dp'), 'tm'), parts along dimension 0
- mean_error: float32 [2], P('parts'), parts along dimension 0
- direction: float32 [640, 2048], P('parts', 'tm'), parts along dimension 0
- back_pre: bfloat16 [16, 512, 2048], P(('parts', 'dp'), 'tm'), parts along dimension 0
There are 2 independent parts, one for each index of `parts`. A program takes and returns all parts, laid end to end along the dimension named above; an argument that names none is the same for every part. Nothing has to cross between parts.
All inputs are finite; a program needn't handle non-finite values.
Results may differ from a plain program's by a relative error of at most 0.0066.
Values may be sent and summed in bfloat16 or wider, within the bound.
A program may use at most 64 MiB of HBM per device.

v0:
```python
import jax
import jax.numpy as jnp
from jax import lax
from jax.sharding import PartitionSpec as P

GW = 64
KERNEL = 5
CH = 2048
KW = 320


beta_one = 0.9
beta_two = 0.999
adam_eps = 1e-08
decay_rate = 0.1
rms_eps = 1e-06
step_count = 100
block_groups = 4


def extended(array, sides, width):
    for axis, dim in sides:
        peers, length = (lax.axis_size(axis), array.shape[dim])
        up = [(i, (i + 1) % peers) for i in range(peers - 1)]
        down = [(j, i) for i, j in up]
        last = lax.slice_in_dim(array, length - width, length, axis=dim)
        initial = lax.slice_in_dim(array, 0, width, axis=dim)
        before = lax.ppermute(last, axis, up)
        after = lax.ppermute(initial, axis, down)
        array = jnp.concatenate([before, array, after], axis=dim)
    return array


def stacked_taps(piece, kernel, length, flipped):
    batch_rows = piece.shape[0]
    groups_here = piece.shape[2] // GW
    slots = []
    for offset in range(kernel):
        start = kernel - 1 - offset if flipped else offset
        slots.append(piece[:, start : start + length].reshape(batch_rows, length, groups_here, GW))
    return jnp.concatenate(slots, axis=3)


def grouped_conv(padded, table, length, flipped):
    batch_rows = padded.shape[0]
    channels = padded.shape[2]
    kernel = table.shape[0] // GW
    block_width = block_groups * GW
    block_count = channels // block_width

    def one_block(index, result):
        begin = index * block_width
        piece = lax.dynamic_slice_in_dim(padded, begin, block_width, 2)
        columns = stacked_taps(piece, kernel, length, flipped)
        table_part = lax.dynamic_slice_in_dim(table, begin, block_width, 1).reshape(
            kernel * GW, block_groups, GW
        )
        product = jnp.einsum(
            "stgq,qgo->stgo", columns, table_part, preferred_element_type=jnp.float32
        )
        return lax.dynamic_update_slice_in_dim(
            result, product.reshape(batch_rows, length, block_width), begin, 2
        )

    start_value = jnp.zeros((batch_rows, length, channels), jnp.float32)
    return lax.fori_loop(0, block_count, one_block, start_value)


def grouped_gradient(padded_signal, padded_mixed, back_pre, error_bf, kernel, length):
    batch_rows = padded_signal.shape[0]
    channels = padded_signal.shape[2]
    block_width = block_groups * GW
    block_count = channels // block_width

    def one_block(index, result):
        begin = index * block_width
        signal_piece = lax.dynamic_slice_in_dim(padded_signal, begin, block_width, 2)
        mixed_piece = lax.dynamic_slice_in_dim(padded_mixed, begin, block_width, 2)
        back_piece = lax.dynamic_slice_in_dim(back_pre, begin, block_width, 2).reshape(
            batch_rows, length, block_groups, GW
        )
        error_piece = lax.dynamic_slice_in_dim(error_bf, begin, block_width, 2).reshape(
            batch_rows, length, block_groups, GW
        )
        signal_cols = stacked_taps(signal_piece, kernel, length, False)
        mixed_cols = stacked_taps(mixed_piece, kernel, length, True)
        encoder_part = jnp.einsum(
            "stgq,stgo->qgo", signal_cols, back_piece, preferred_element_type=jnp.float32
        )
        decoder_part = jnp.einsum(
            "stgq,stgi->qgi", mixed_cols, error_piece, preferred_element_type=jnp.float32
        )
        decoder_part = (
            decoder_part.reshape(kernel, GW, block_groups, GW)
            .transpose(0, 3, 2, 1)
            .reshape(kernel * GW, block_groups, GW)
        )
        summed = (encoder_part + decoder_part).reshape(kernel * GW, block_width)
        return lax.dynamic_update_slice_in_dim(result, summed, begin, 1)

    start_value = jnp.zeros((kernel * GW, channels), jnp.float32)
    return lax.fori_loop(0, block_count, one_block, start_value)


def silu_slope(pre):
    sigma = jax.nn.sigmoid(pre)
    return sigma * (1.0 + pre * (1.0 - sigma))


def adam_direction(grad_part, square_total, entries, weight_part, first_part, second_part):
    rms_value = jnp.sqrt(square_total / entries + rms_eps)
    factor = jnp.minimum(1.0, 1.0 / rms_value)
    clipped = grad_part * factor
    first_new = beta_one * first_part + (1.0 - beta_one) * clipped
    second_new = beta_two * second_part + (1.0 - beta_two) * clipped * clipped
    first_hat = first_new / (1.0 - beta_one**step_count)
    second_hat = second_new / (1.0 - beta_two**step_count)
    return first_hat / (jnp.sqrt(second_hat) + adam_eps) + decay_rate * weight_part


def on_device(signal, weight, first_moment, second_moment, shuffle):
    batch_rows = signal.shape[0]
    local_rows = signal.shape[1]
    channels = signal.shape[2]
    margin = (KERNEL - 1) // 2
    full_weight = lax.all_gather(weight.astype(jnp.bfloat16), "tm", axis=1, tiled=True)
    flipped_weight = (
        full_weight.reshape(KERNEL, GW, channels // GW, GW)
        .transpose(0, 3, 2, 1)
        .reshape(KERNEL * GW, channels)
    )
    inverse = (
        jnp.zeros((channels,), jnp.int32).at[shuffle].set(jnp.arange(channels, dtype=jnp.int32))
    )
    padded_signal = extended(signal, (("tm", 1),), margin)
    pre = grouped_conv(padded_signal, full_weight, local_rows, False)
    mixed = jnp.take(jax.nn.silu(pre).astype(jnp.bfloat16), shuffle, axis=2)
    padded_mixed = extended(mixed, (("tm", 1),), margin)
    decoded = grouped_conv(padded_mixed, flipped_weight, local_rows, True)
    error = decoded - signal.astype(jnp.float32)
    error_bf = error.astype(jnp.bfloat16)
    square_sum = lax.psum(jnp.sum(error * error), ("tm", "dp"))
    element_count = batch_rows * lax.axis_size("dp") * local_rows * lax.axis_size("tm") * channels
    mean_error = (square_sum / element_count).reshape(1)
    padded_error = extended(error_bf, (("tm", 1),), margin)
    back_mixed = grouped_conv(padded_error, full_weight, local_rows, False)
    back_pre = (jnp.take(back_mixed, inverse, axis=2) * silu_slope(pre)).astype(jnp.bfloat16)
    gradient = grouped_gradient(padded_signal, padded_mixed, back_pre, error_bf, KERNEL, local_rows)
    owned = lax.psum_scatter(gradient, "tm", scatter_dimension=1, tiled=True)
    owned = lax.psum(owned.astype(jnp.bfloat16), "dp").astype(jnp.float32)
    square_total = lax.psum(jnp.sum(owned * owned), "tm")
    direction = adam_direction(owned, square_total, KW * CH, weight, first_moment, second_moment)
    return (decoded.astype(jnp.bfloat16), mean_error, direction, back_pre)


def solution(mesh):
    return jax.shard_map(
        on_device,
        mesh=mesh,
        in_specs=(
            P(("parts", "dp"), "tm", None),
            P("parts", "tm"),
            P("parts", "tm"),
            P("parts", "tm"),
            P(),
        ),
        out_specs=(
            P(("parts", "dp"), "tm", None),
            P("parts"),
            P("parts", "tm"),
            P(("parts", "dp"), "tm", None),
        ),
        check_vma=False,
    )
```

profile of v0, /device:TPU:0, one launch (start us, length us, event | category | flops | bytes accessed | tf_op | source)
XLA Modules:
  0.0 463.2 jit_solution(3535167079590880760)
XLA Ops:
  7.2 1.9 convert_element_type.24
  10.1 4.9 %collective-permute-start = (bf16[2,2,2048]{2,1,0:T(2,128)(2,1)S(1)}, bf16[2,2,2048]{2,1,0:T(2,128)(2,1)S(1)}, u32[]{:S(2)}, u32[]{:S(2)}) collective-permute-start(bf16[2,2,2048]{2,1,0:T(2,128)(2,1)S(1)} %get-tuple-element.481), channel_id=1, source_target_pairs={{0,4},{4,8},{8,12},{1,5},{5,9},{9,13},{2,6},{6,10},{10,14},{3,7},{... | collective-permute-start | bytes 49160 | tf_op jit(solution)/shard_map/ppermute | solution.py:28
  18.5 8.0 %scatter_custom_fusion = s32[2048]{0:T(1024)S(1)} fusion(s32[2048]{0:T(1024)S(1)} %get-tuple-element.483, s32[2048]{0:T(1024)S(1)} %iota.3, s32[]{:T(128)} %constant.160.clone.1), kind=kCustom, calls=%fused_computation.102 | custom fusion | bytes 8196 | tf_op jit(solution)/shard_map/scatter | solution.py:133
  29.3 2.7 pad_maximum_fusion
  32.0 13.6 %all-gather.2.cloned.1.call-done = bf16[320,2048]{1,0:T(8,128)(2,1)} async-done(((bf16[320,512]{1,0:T(8,128)(2,1)}), bf16[320,2048]{1,0:T(8,128)(2,1)}) %all-gather.2.cloned.1.call-update) | async-done | bytes 1310736 | tf_op jit(solution)/shard_map/all_gather | solution.py:126
  45.6 2.5 copy.134
  49.8 21.5 %while.52 = (s32[]{:T(128)}, f32[2,128,2048]{1,0,2:T(2,128)}, bf16[320,2048]{0,1:T(8,128)(2,1)}, bf16[2,132,2048]{1,2,0:T(8,128)(2,1)S(1)}, s32[]{:T(128)}, /*in...) while((s32[]{:T(128)}, f32[2,128,2048]{1,0,2:T(2,128)}, ...), condition=%wide.region_1.0_spmd, body=%wide.region_0.0_spmd.sunk | while | flops 41943048 | bytes 5079279 | solution.py:66
  71.3 3.4 multiply_convert_fusion
  74.8 13.9 %gather_fusion = bf16[2048,2,128]{2,1,0:T(2,128)(2,1)} fusion(bf16[2,128,2048]{1,0,2:T(2,128)(2,1)S(1)} %multiply_convert_fusion, s32[2048]{0:T(1024)S(1)} %get-tuple-element.484), kind=kCustom, calls=%fused_computation | custom fusion | bytes 2105344 | tf_op jit(solution)/shard_map/jit(_take)/gather | solution.py:137
  88.7 9.8 %fusion.6 = bf16[2,128,2048]{1,0,2:T(2,128)(2,1)S(1)} fusion(bf16[2048,2,128]{2,1,0:T(2,128)(2,1)} %gather_fusion, pred[2048]{0:T(1024)(128)(4,1)S(1)} %compare_and_fusion.1), kind=kLoop, calls=%fused_computation.82 | loop fusion | flops 524288 | bytes 2099200 | tf_op jit(solution)/shard_map/jit(_take)/select_n | solution.py:137
  98.4 2.8 fusion.21
  101.2 2.6 copy.137
  103.8 2.7 collective-permute-start.2
  106.5 2.6 copy.138
  110.5 4.9 %reshape.279 = bf16[5,64,32,64]{3,2,1,0:T(8,128)(2,1)} reshape(bf16[320,2048]{1,0:T(8,128)(2,1)} %all-gather.2.cloned.1.call-done) | data formatting | bytes 2621440 | tf_op jit(solution)/shard_map/reshape | solution.py:128
  115.5 5.6 %copy.160 = bf16[5,64,32,64]{1,0,3,2:T(8,128)(2,1)} copy(bf16[5,64,32,64]{1,2,3,0:T(8,128)(2,1)} %bitcast.215) | data formatting | bytes 2621440 | tf_op jit(solution)/shard_map/while | solution.py:66
  121.0 5.8 %reshape.314 = bf16[320,2048]{0,1:T(8,128)(2,1)} reshape(bf16[5,64,32,64]{1,0,3,2:T(8,128)(2,1)} %copy.160) | data formatting | bytes 2621440 | tf_op jit(solution)/shard_map/while | solution.py:66
  126.9 2.1 copy.139
  129.0 2.1 copy.140
  131.0 7.2 %pad_maximum_fusion.1 = bf16[2,132,2048]{1,0,2:T(2,128)(2,1)S(1)} fusion(bf16[2,2,2048]{1,0,2:T(2,128)(2,1)} %copy.140, bf16[2,128,2048]{1,0,2:T(2,128)(2,1)S(1)} %fusion.6, bf16[2,2,2048]{1,0,2:T(2,128)(2,1)} %copy.139), kind=kLoop, calls=%fused_computation.72 | loop fusion | flops 3244032 | bytes 2162688 | tf_op jit(solution)/shard_map/concatenate | solution.py:30
  141.4 33.2 %while.53 = (s32[]{:T(128)}, f32[2,128,2048]{2,1,0:T(8,128)}, bf16[320,2048]{0,1:T(8,128)(2,1)}, bf16[2,132,2048]{1,2,0:T(8,128)(2,1)}, s32[]{:T(128)}, /*index=...) while((s32[]{:T(128)}, f32[2,128,2048]{2,1,0:T(8,128)}, ...), condition=%wide.region_3.4_spmd, body=%wide.region_2.0_spmd.sunk | while | flops 41943048 | bytes 5603567 | solution.py:66
  141.4 2.0 constant_dynamic-slice_fusion.42
  149.9 2.0 constant_dynamic-slice_fusion.42
  154.1 1.9 constant_dynamic-slice_fusion.42
  162.4 1.9 constant_dynamic-slice_fusion.42
  166.5 1.8 constant_dynamic-slice_fusion.42
  174.6 4.6 fusion.5
  179.3 4.5 collective-permute-start.4
  185.4 4.1 collective-permute-done.5
  192.4 37.6 %while.54 = (s32[]{:T(128)}, f32[2,128,2048]{1,0,2:T(2,128)}, bf16[320,2048]{0,1:T(8,128)(2,1)}, bf16[2,132,2048]{2,1,0:T(8,128)(2,1)}, s32[]{:T(128)}, /*index=...) while((s32[]{:T(128)}, f32[2,128,2048]{1,0,2:T(2,128)}, ...), condition=%wide.region_8.9_spmd, body=%wide.region_7.8_spmd.sunk | while | flops 41943048 | bytes 6389999 | solution.py:66
  201.7 1.9 constant_dynamic-slice_fusion.44
  211.2 1.9 constant_dynamic-slice_fusion.44
  230.0 16.0 %gather_fusion.1 = f32[2048,2,128]{2,1,0:T(2,128)} fusion(f32[2,128,2048]{1,0,2:T(2,128)} %get-tuple-element.352, s32[2048]{0:T(1024)S(1)} %fusion.17), kind=kCustom, calls=%fused_computation.1 | custom fusion | bytes 4202496 | tf_op jit(solution)/shard_map/jit(_take)/gather | solution.py:147
  246.0 11.4 %fusion.4 = bf16[2,128,2048]{1,0,2:T(2,128)(2,1)} fusion(f32[2048,2,128]{2,1,0:T(2,128)} %gather_fusion.1, f32[2,128,2048]{1,0,2:T(2,128)} %get-tuple-element.350, pred[2048]{0:T(1024)(128)(4,1)S(1)} %compare_and_fusion), kind=kLoop, calls=%fused_computation.74 | loop fusion | flops 5242880 | bytes 5244928 | tf_op jit(solution)/shard_map/convert_element_type | solution.py:147
  259.2 92.0 %while.55 = (s32[]{:T(128)}, f32[320,2048]{1,0:T(8,128)}, bf16[2,128,2048]{1,0,2:T(2,128)(2,1)}, bf16[2,132,2048]{1,2,0:T(8,128)(2,1)S(1)}, bf16[2,128,2048]{2,1...) while((s32[]{:T(128)}, f32[320,2048]{1,0:T(8,128)}, ...), condition=%wide.region_10.11_spmd, body=%wide.region_9.10_spmd.sunk | while | flops 83968008 | bytes 12124419 | solution.py:102
  259.2 2.6 constant_dynamic-slice_fusion.46
  270.9 2.4 constant_dynamic-slice_fusion.46
  282.3 2.6 constant_dynamic-slice_fusion.46
  293.9 2.5 constant_dynamic-slice_fusion.46
  305.4 2.4 constant_dynamic-slice_fusion.46
  316.9 2.5 constant_dynamic-slice_fusion.46
  328.4 2.4 constant_dynamic-slice_fusion.46
  339.8 2.4 constant_dynamic-slice_fusion.46
  351.3 51.0 %reduce-scatter.2.cloned.1.call-done = f32[320,512]{1,0:T(8,128)} async-done(((f32[320,2048]{1,0:T(8,128)}), f32[320,512]{1,0:T(8,128)}) %reduce-scatter.2.cloned.1.call-update) | async-done | bytes 655376 | tf_op jit(solution)/shard_map/reduce_scatter | solution.py:149
  402.3 1.9 convert_element_type.30
  404.2 32.6 %psum.21 = f32[]{:T(128)} all-reduce(f32[]{:T(128)} %get-tuple-element.475), channel_id=1, replica_groups=mesh['parts'=2,'tm'=4,'dp'=4] {'tm','dp'}, use_global_device_ids=true, to_apply=%region_5.6 | all-reduce | flops 1 | bytes 8 | tf_op jit(solution)/shard_map/psum | solution.py:142
  439.3 2.0 copy.153
  441.3 12.2 %psum.23 = f32[]{:T(128)} all-reduce(f32[]{:T(128)} %fusion.12), channel_id=1, replica_groups=mesh['parts'=2,'tm'=4,'dp'=4] {'tm'}, use_global_device_ids=true, to_apply=%region_14.15 | all-reduce | flops 1 | bytes 8 | tf_op jit(solution)/shard_map/psum | solution.py:151
  (496 shorter events, 171.7 us)
Async XLA Ops:
  7.2 10.6 %copy-start.2 = (bf16[2,128,2048]{2,1,0:T(8,128)(2,1)S(1)}, bf16[2,128,2048]{2,1,0:T(8,128)(2,1)}, u32[]{:S(2)}) copy-start(bf16[2,128,2048]{2,1,0:T(8,128)(2,1)} %param.13) | copy-start | bytes 3145732
  7.2 38.4 %all-gather.2.cloned.1.call-start = ((), (), s32[]{:S(2)}) async-start(), calls=%async_computation.1 | async-start | bytes 1638400 | tf_op jit(solution)/shard_map/all_gather | solution.py:126
  9.2 393.2 %reduce-scatter.2.cloned.1.call-start = ((), (), s32[]{:S(2)}) async-start(), calls=%async_computation.2 | async-start | bytes 3276800 | tf_op jit(solution)/shard_map/reduce_scatter | solution.py:149
  10.1 16.4 %collective-permute-start = (bf16[2,2,2048]{2,1,0:T(2,128)(2,1)S(1)}, bf16[2,2,2048]{2,1,0:T(2,128)(2,1)S(1)}, u32[]{:S(2)}, u32[]{:S(2)}) collective-permute-start(bf16[2,2,2048]{2,1,0:T(2,128)(2,1)S(1)} %get-tuple-element.481), channel_id=1, source_target_pairs={{0,4},{4,8},{8,12},{1,5},{5,9},{9,13},{2,6},{6,10},{10,14},{3,7},{... | collective-permute-start | bytes 49160 | tf_op jit(solution)/shard_map/ppermute | solution.py:28
  15.1 12.8 %collective-permute-start.1 = (bf16[2,2,2048]{2,1,0:T(2,128)(2,1)S(1)}, bf16[2,2,2048]{2,1,0:T(2,128)(2,1)S(1)}, u32[]{:S(2)}, u32[]{:S(2)}) collective-permute-start(bf16[2,2,2048]{2,1,0:T(2,128)(2,1)S(1)} %get-tuple-element.482), channel_id=1, source_target_pairs={{4,0},{8,4},{12,8},{5,1},{9,5},{13,9},{6,2},{10,6},{14,10},{7,3},{... | collective-permute-start | bytes 49160 | tf_op jit(solution)/shard_map/ppermute | solution.py:29
  103.8 23.1 %collective-permute-start.2 = (bf16[2,2,2048]{2,1,0:T(2,128)(2,1)S(1)}, bf16[2,2,2048]{2,1,0:T(2,128)(2,1)S(1)}, u32[]{:S(2)}, u32[]{:S(2)}) collective-permute-start(bf16[2,2,2048]{2,1,0:T(2,128)(2,1)S(1)} %copy.137), channel_id=1, source_target_pairs={{0,4},{4,8},{8,12},{1,5},{5,9},{9,13},{2,6},{6,10},{10,14},{3,7},{... | collective-permute-start | bytes 49160 | tf_op jit(solution)/shard_map/ppermute | solution.py:28
  109.0 19.9 %collective-permute-start.3 = (bf16[2,2,2048]{2,1,0:T(2,128)(2,1)S(1)}, bf16[2,2,2048]{2,1,0:T(2,128)(2,1)S(1)}, u32[]{:S(2)}, u32[]{:S(2)}) collective-permute-start(bf16[2,2,2048]{2,1,0:T(2,128)(2,1)S(1)} %copy.138), channel_id=1, source_target_pairs={{4,0},{8,4},{12,8},{5,1},{9,5},{13,9},{6,2},{10,6},{14,10},{7,3},{... | collective-permute-start | bytes 49160 | tf_op jit(solution)/shard_map/ppermute | solution.py:29
  179.2 13.2 %copy-start = (bf16[2,128,2048]{2,1,0:T(8,128)(2,1)}, bf16[2,128,2048]{2,1,0:T(8,128)(2,1)S(1)}, u32[]{:S(2)}) copy-start(bf16[2,128,2048]{2,1,0:T(8,128)(2,1)S(1)} %get-tuple-element.759) | copy-start | bytes 3145732
  179.3 6.1 %collective-permute-start.4 = (bf16[2,2,2048]{2,1,0:T(2,128)(2,1)S(1)}, bf16[2,2,2048]{2,1,0:T(2,128)(2,1)S(1)}, u32[]{:S(2)}, u32[]{:S(2)}) collective-permute-start(bf16[2,2,2048]{2,1,0:T(2,128)(2,1)S(1)} %get-tuple-element.477), channel_id=1, source_target_pairs={{0,4},{4,8},{8,12},{1,5},{5,9},{9,13},{2,6},{6,10},{10,14},{3,7},{... | collective-permute-start | bytes 49160 | tf_op jit(solution)/shard_map/ppermute | solution.py:28
  183.8 5.6 %collective-permute-start.5 = (bf16[2,2,2048]{2,1,0:T(2,128)(2,1)S(1)}, bf16[2,2,2048]{2,1,0:T(2,128)(2,1)S(1)}, u32[]{:S(2)}, u32[]{:S(2)}) collective-permute-start(bf16[2,2,2048]{2,1,0:T(2,128)(2,1)S(1)} %get-tuple-element.478), channel_id=1, source_target_pairs={{4,0},{8,4},{12,8},{5,1},{9,5},{13,9},{6,2},{10,6},{14,10},{7,3},{... | collective-permute-start | bytes 49160 | tf_op jit(solution)/shard_map/ppermute | solution.py:29
  351.2 88.1 %copy-start.1 = (bf16[2,128,2048]{1,0,2:T(2,128)(2,1)S(1)}, bf16[2,128,2048]{1,0,2:T(2,128)(2,1)}, u32[]{:S(2)}) copy-start(bf16[2,128,2048]{1,0,2:T(2,128)(2,1)} %get-tuple-element.805) | copy-start | bytes 3145732
  351.3 102.9 %copy-start.3 = (f32[320,512]{1,0:T(8,128)S(1)}, f32[320,512]{1,0:T(8,128)}, u32[]{:S(2)}) copy-start(f32[320,512]{1,0:T(8,128)} %param.14) | copy-start | bytes 1966084
  351.3 102.9 %copy-start.5 = (f32[320,512]{1,0:T(8,128)S(1)}, f32[320,512]{1,0:T(8,128)}, u32[]{:S(2)}) copy-start(f32[320,512]{1,0:T(8,128)} %param.16) | copy-start | bytes 1966084
  351.3 102.9 %copy-start.6 = (f32[320,512]{1,0:T(8,128)S(1)}, f32[320,512]{1,0:T(8,128)}, u32[]{:S(2)}) copy-start(f32[320,512]{1,0:T(8,128)} %param.15) | copy-start | bytes 1966084
  351.3 86.2 %all-reduce.2.cloned.1.call-start = ((), (), s32[]{:S(2)}) async-start(), calls=%async_computation.3 | async-start | bytes 655360 | tf_op jit(solution)/shard_map/psum | solution.py:150
  437.5 16.7 %copy-start.4 = (bf16[320,512]{1,0:T(8,128)(2,1)S(1)}, bf16[320,512]{1,0:T(8,128)(2,1)}, u32[]{:S(2)}) copy-start(bf16[320,512]{1,0:T(8,128)(2,1)} %all-reduce.2.cloned.1.call-done) | copy-start | bytes 983044
Sparse Core Ops, SparseCore 0:
  10.2 35.3 all-gather.1
  351.4 50.9 reduce-scatter.1
  405.3 32.0 all-reduce.1
where the time goes:
time: 467 us; the launch traced here: 463 us
  local copies, waits for them, and re-layouts  246 us (53%)
  waiting for transfers between devices  68.8 us (15%)
  other arithmetic  48.7 us (10%)
  blocking collectives  44.8 us (10%)
  matrix products  19.7 us (4%)
  starting transfers between devices  16.5 us (4%)
  between operations  16.5 us (4%)
    slice x32, local copies, waits for them, and re-layouts, stacked_taps(): piece[:, start:start + length].reshape(batch_rows, length, groups_here, GW)  52.2 us
    reduce_scatter x1, waiting for transfers between devices, on_device(): owned = lax.psum_scatter(gradient, 'tm', scatter_dimension=1, tiled=True)  51 us
    psum x1, blocking collectives, on_device(): square_sum = lax.psum(jnp.sum(error * error), ('tm', 'dp'))  32.6 us
    while x200, local copies, waits for them, and re-layouts  28.8 us
    dynamic_slice x24, local copies, waits for them, and re-layouts, one_block(): lax.dynamic_slice_in_dim(table, begin, block_width, 1)  22.9 us
    dynamic_update_slice x32, local copies, waits for them, and re-layouts, one_block(): lax.dynamic_update_slice_in_dim(result, product.reshape(batch_rows, lengt...  21.8 us
    gather x1, local copies, waits for them, and re-layouts, on_device(): jnp.take(back_mixed, inverse, axis=2) * silu_slope(pre)  16 us
    while x4, local copies, waits for them, and re-layouts, grouped_conv(): return lax.fori_loop(0, block_count, one_block, start_value)  15.6 us
  transfers between devices with their start and end apart: 9, of which 3 were waited for; matrix products, arithmetic and copies ran while one was open for 8% of the time, Pallas kernels for 0%

commit v1 on v0

v1 whole, which is shorter than its diff:
```python
import functools

import jax
import jax.numpy as jnp
from jax import lax
from jax.experimental import pallas as pl
from jax.experimental.pallas import tpu as pltpu
from jax.sharding import PartitionSpec as P

GW = 64
KERNEL = 5
CH = 2048
KW = 320
WIDE = 256
HALO = 8

beta_one = 0.9
beta_two = 0.999
adam_eps = 1e-08
decay_rate = 0.1
rms_eps = 1e-06
step_count = 100

TN = (((0,), (0,)), ((), ()))
NT = (((1,), (1,)), ((), ()))


def shifted(value, amount):
    rows = value.shape[0]
    return value if amount % rows == 0 else pltpu.roll(value, amount % rows, 0)


def local_part(value, windows, length):
    step = length + 2 * HALO
    return jnp.concatenate(
        [value[w * step + HALO : w * step + HALO + length] for w in range(windows)], axis=0
    )


def spread_part(value, windows, length):
    blank = jnp.zeros((HALO, value.shape[1]), value.dtype)
    pieces = []
    for w in range(windows):
        pieces += [blank, value[w * length : (w + 1) * length], blank]
    return jnp.concatenate(pieces, axis=0)


def diagonal(value):
    lane = lax.broadcasted_iota(jnp.int32, (GW, WIDE), 1) // GW
    picked = value[:GW]
    for j in range(1, WIDE // GW):
        picked = jnp.where(lane == j, value[j * GW : (j + 1) * GW], picked)
    return picked


def compute_kernel(
    windows, length, sig_ref, w_ref, shuffle_ref, rec_ref, back_ref, grad_ref, square_ref,
    onehot, table, pre, act, back, partial,
):
    channels = sig_ref.shape[1]
    blocks = channels // WIDE
    rows = sig_ref.shape[0]
    step = length + 2 * HALO
    me, peers = lax.axis_index("tm"), lax.axis_size("tm")
    place = lax.broadcasted_iota(jnp.int32, (rows, WIDE), 0)
    inner = lax.rem(place, step)
    low = jnp.where(me == 0, HALO, 0)
    high = jnp.where(me == peers - 1, HALO + length, step)
    inside = jnp.logical_and(inner >= low, inner < high)
    block_mask = (
        lax.broadcasted_iota(jnp.int32, (WIDE, WIDE), 0) // GW
        == lax.broadcasted_iota(jnp.int32, (WIDE, WIDE), 1) // GW
    )
    square_ref[...] = jnp.zeros_like(square_ref)

    def encode(index, carry):
        cols = pl.ds(pl.multiple_of(index * WIDE, WIDE), WIDE)
        for k in range(KERNEL):
            taps = w_ref[k * GW : (k + 1) * GW, cols].astype(jnp.float32)
            tiled = jnp.concatenate([taps] * (WIDE // GW), axis=0)
            table[index, k * WIDE : (k + 1) * WIDE, :] = jnp.where(block_mask, tiled, 0.0).astype(
                jnp.bfloat16
            )
        x = sig_ref[:, cols].astype(jnp.float32)
        stack = jnp.concatenate(
            [shifted(x, 2 - k).astype(jnp.bfloat16) for k in range(KERNEL)], axis=1
        )
        value = jnp.dot(stack, table[index], preferred_element_type=jnp.float32)
        pre[:, cols] = local_part(value, windows, length)
        active = value / (1.0 + jnp.exp(-value))
        act[:, cols] = jnp.where(inside, active, 0.0).astype(jnp.bfloat16)
        return carry

    lax.fori_loop(0, blocks, encode, 0)

    def decode(index, carry):
        cols = pl.ds(pl.multiple_of(index * WIDE, WIDE), WIDE)
        source = lax.broadcasted_iota(jnp.int32, (channels, WIDE), 0)
        onehot[:, cols] = jnp.where(source == shuffle_ref[:, cols], 1.0, 0.0).astype(jnp.bfloat16)
        mixed = jnp.dot(act[...], onehot[:, cols], preferred_element_type=jnp.float32)
        decoded = jnp.zeros((rows, WIDE), jnp.float32)
        own_mixed = []
        for k in range(KERNEL):
            moved = shifted(mixed, k - 2)
            own_mixed.append(local_part(moved, windows, length).astype(jnp.bfloat16))
            decoded += lax.dot_general(
                moved.astype(jnp.bfloat16),
                table[index, k * WIDE : (k + 1) * WIDE, :],
                NT,
                preferred_element_type=jnp.float32,
            )
        error = jnp.where(inside, decoded - sig_ref[:, cols].astype(jnp.float32), 0.0)
        own_decoded = local_part(decoded, windows, length).astype(jnp.bfloat16)
        for w in range(windows):
            rec_ref[w, :, cols] = own_decoded[w * length : (w + 1) * length]
        own_error = local_part(error, windows, length)
        square_ref[...] += (own_error * own_error).reshape(-1, 8, WIDE).sum(axis=0)
        stack = jnp.concatenate(
            [shifted(error, 2 - k).astype(jnp.bfloat16) for k in range(KERNEL)], axis=1
        )
        value = jnp.dot(stack, table[index], preferred_element_type=jnp.float32)
        back[:, cols] = local_part(value, windows, length).astype(jnp.bfloat16)
        product = lax.dot_general(
            own_error.astype(jnp.bfloat16),
            jnp.concatenate(own_mixed, axis=1),
            TN,
            preferred_element_type=jnp.float32,
        )
        for k in range(KERNEL):
            partial[k * GW : (k + 1) * GW, cols] = diagonal(product[:, k * WIDE : (k + 1) * WIDE])
        return carry

    lax.fori_loop(0, blocks, decode, 0)

    def finish(index, carry):
        start = pl.multiple_of(index * WIDE, WIDE)
        cols = pl.ds(start, WIDE)
        restored = lax.dot_general(
            back[...], onehot[pl.ds(start, WIDE), :], NT, preferred_element_type=jnp.float32
        )
        value = pre[:, cols]
        sigma = 1.0 / (1.0 + jnp.exp(-value))
        own = (restored * (sigma * (1.0 + value * (1.0 - sigma)))).astype(jnp.bfloat16)
        for w in range(windows):
            back_ref[w, :, cols] = own[w * length : (w + 1) * length]
        wide = spread_part(own.astype(jnp.float32), windows, length)
        stack = jnp.concatenate(
            [shifted(wide, k - 2).astype(jnp.bfloat16) for k in range(KERNEL)], axis=1
        )
        product = lax.dot_general(
            sig_ref[:, cols], stack, TN, preferred_element_type=jnp.float32
        )
        for k in range(KERNEL):
            taken = slice(k * GW, (k + 1) * GW)
            total = partial[taken, cols] + diagonal(product[:, k * WIDE : (k + 1) * WIDE])
            grad_ref[taken, cols] = total.astype(grad_ref.dtype)
        return carry

    lax.fori_loop(0, blocks, finish, 0)


def local_step(signal, weight, shuffle, before, after):
    windows, length, channels = signal.shape
    wide = jnp.concatenate([before, signal, after], axis=1)
    rows = windows * (length + 2 * HALO)
    vmem = pl.BlockSpec(memory_space=pltpu.VMEM)
    own = windows * length
    return pl.pallas_call(
        functools.partial(compute_kernel, windows, length),
        out_shape=(
            jax.ShapeDtypeStruct(signal.shape, jnp.bfloat16),
            jax.ShapeDtypeStruct(signal.shape, jnp.bfloat16),
            jax.ShapeDtypeStruct((KERNEL * GW, channels), jnp.bfloat16),
            jax.ShapeDtypeStruct((8, WIDE), jnp.float32),
        ),
        in_specs=[vmem] * 3,
        out_specs=(vmem,) * 4,
        scratch_shapes=[
            pltpu.VMEM((channels, channels), jnp.bfloat16),
            pltpu.VMEM((channels // WIDE, KERNEL * WIDE, WIDE), jnp.bfloat16),
            pltpu.VMEM((own, channels), jnp.float32),
            pltpu.VMEM((rows, channels), jnp.bfloat16),
            pltpu.VMEM((own, channels), jnp.bfloat16),
            pltpu.VMEM((KERNEL * GW, channels), jnp.float32),
        ],
        compiler_params=pltpu.CompilerParams(vmem_limit_bytes=48 * 1024 * 1024),
    )(wide.reshape(rows, channels), weight, shuffle.reshape(1, channels))


def adam_direction(grad_part, square_total, entries, weight_part, first_part, second_part):
    rms_value = jnp.sqrt(square_total / entries + rms_eps)
    factor = jnp.minimum(1.0, 1.0 / rms_value)
    clipped = grad_part * factor
    first_new = beta_one * first_part + (1.0 - beta_one) * clipped
    second_new = beta_two * second_part + (1.0 - beta_two) * clipped * clipped
    first_hat = first_new / (1.0 - beta_one**step_count)
    second_hat = second_new / (1.0 - beta_two**step_count)
    return first_hat / (jnp.sqrt(second_hat) + adam_eps) + decay_rate * weight_part


def on_device(signal, weight, first_moment, second_moment, shuffle):
    windows, length, channels = signal.shape
    peers = lax.axis_size("tm")
    up = [(i, i + 1) for i in range(peers - 1)]
    down = [(j, i) for i, j in up]
    before = lax.ppermute(signal[:, length - HALO :], "tm", up)
    after = lax.ppermute(signal[:, :HALO], "tm", down)
    full_weight = lax.all_gather(weight.astype(jnp.bfloat16), "tm", axis=1, tiled=True)
    decoded, back_pre, gradient, squares = local_step(signal, full_weight, shuffle, before, after)
    square_sum = lax.psum(jnp.sum(squares), ("tm", "dp"))
    element_count = windows * lax.axis_size("dp") * length * peers * channels
    mean_error = (square_sum / element_count).reshape(1)
    owned = lax.psum_scatter(gradient, "tm", scatter_dimension=1, tiled=True)
    owned = lax.psum(owned, "dp").astype(jnp.float32)
    square_total = lax.psum(jnp.sum(owned * owned), "tm")
    direction = adam_direction(owned, square_total, KW * CH, weight, first_moment, second_moment)
    return (decoded, mean_error, direction, back_pre)


def solution(mesh):
    return jax.shard_map(
        on_device,
        mesh=mesh,
        in_specs=(
            P(("parts", "dp"), "tm", None),
            P("parts", "tm"),
            P("parts", "tm"),
            P("parts", "tm"),
            P(),
        ),
        out_specs=(
            P(("parts", "dp"), "tm", None),
            P("parts"),
            P("parts", "tm"),
            P(("parts", "dp"), "tm", None),
        ),
        check_vma=False,
    )
```

time: 467 us -> 168 us (0.36)
  local copies, waits for them, and re-layouts: 246 us -> 1.35 us
  other arithmetic: 48.7 us -> 6.7 us
  Pallas kernels: 0 us -> 31.5 us
  matrix products: 19.7 us -> 0 us
  starting transfers between devices: 16.5 us -> 6.34 us
  waiting for transfers between devices: 68.8 us -> 61.5 us
    slice x37 -> x1, local copies, waits for them, and re-layouts: 61.1 us -> 0.01 us  [on_device(): before = lax.ppermute(signal[:, length - HALO:], 'tm', up)]
    while x204 -> x0, local copies, waits for them, and re-layouts: 44.4 us -> none
    dynamic_slice x56 -> x0, local copies, waits for them, and re-layouts: 39.4 us -> none  [the longest x24 22.9 us: one_block(): lax.dynamic_slice_in_dim(table, begin, block_width, 1)]
    pallas_call x0 -> x1, Pallas kernels: none -> 31.5 us  [local_step(): pl.pallas_call(functools.partial(compute_kernel, windows, length), out_sh...]
    gather x2 -> x0, local copies, waits for them, and re-layouts: 29.9 us -> none  [the longest x1 16 us: on_device(): jnp.take(back_mixed, inverse, axis=2) * silu_slope(pre)]
    dynamic_update_slice x48 -> x0, local copies, waits for them, and re-layouts: 29.4 us -> none  [the longest x32 21.8 us: one_block(): lax.dynamic_update_slice_in_dim(result, product.reshape(batch_rows, lengt...]
    convert_element_type x4 -> x0, other arithmetic: 21.3 us -> none  [the longest x1 11.4 us: on_device(): (jnp.take(back_mixed, inverse, axis=2) * silu_slope(pre)).astype(jnp.bflo...]
    reduce_scatter x1, waiting for transfers between devices: 51 us -> 30.3 us  [on_device(): owned = lax.psum_scatter(gradient, 'tm', scatter_dimension=1, tiled=True)]
  transfers between devices with their start and end apart: 9 -> 5, of which waited for: 3 -> 5; matrix products, arithmetic and copies ran while one was open for 8% -> 0% of each run, Pallas kernels for 0% -> 0%
where the time goes in v1:
time: 168 us
  waiting for transfers between devices  61.5 us (37%)
  blocking collectives  44.1 us (26%)
  Pallas kernels  31.5 us (19%)
  between operations  16.3 us (10%)
  other arithmetic  6.7 us (4%)
  starting transfers between devices  6.34 us (4%)
    psum x1, blocking collectives, on_device(): square_sum = lax.psum(jnp.sum(squares), ('tm', 'dp'))  31.8 us
    pallas_call x1, Pallas kernels, local_step(): pl.pallas_call(functools.partial(compute_kernel, windows, length), out_sh...  31.5 us
    reduce_scatter x1, waiting for transfers between devices, on_device(): owned = lax.psum_scatter(gradient, 'tm', scatter_dimension=1, tiled=True)  30.3 us
    all_gather x1, waiting for transfers between devices, on_device(): lax.all_gather(weight.astype(jnp.bfloat16), 'tm', axis=1, tiled=True)  25.1 us
    psum x1, blocking collectives, on_device(): square_total = lax.psum(jnp.sum(owned * owned), 'tm')  12.3 us
    ppermute x1, starting transfers between devices, on_device(): before = lax.ppermute(signal[:, length - HALO:], 'tm', up)  4.93 us
    ppermute x1, waiting for transfers between devices, on_device(): after = lax.ppermute(signal[:, :HALO], 'tm', down)  4.27 us
  transfers between devices with their start and end apart: 5, of which 5 were waited for; matrix products, arithmetic and copies ran while one was open for 0% of the time, Pallas kernels for 0%

profile of v1, /device:TPU:0, one launch (start us, length us, event | category | flops | bytes accessed | tf_op | source)
XLA Modules:
  0.0 167.8 jit_solution(5665193059278318640)
XLA Ops:
  7.2 0.0 copy-start.3
  7.2 0.0 all-gather.2.cloned.1.call-start
  7.2 1.9 %convert_element_type.6 = bf16[320,512]{1,0:T(8,128)(2,1)} convert(f32[320,512]{1,0:T(8,128)} %param.6) | non-fusion elementwise | flops 163840 | bytes 983040 | tf_op jit(solution)/shard_map/convert_element_type | solution.py:208
  9.2 0.0 all-gather.2.cloned.1.call-update
  9.2 0.0 copy-start.1
  9.2 0.0 reduce-scatter.2.cloned.1.call-start
  9.2 0.0 copy-done.3
  9.3 4.9 %collective-permute-start = (bf16[2,8,2048]{2,1,0:T(8,128)(2,1)S(1)}, bf16[2,8,2048]{2,1,0:T(8,128)(2,1)S(1)}, u32[]{:S(2)}, u32[]{:S(2)}) collective-permute-start(bf16[2,8,2048]{2,1,0:T(8,128)(2,1)S(1)} %get-tuple-element.12), channel_id=1, source_target_pairs={{0,4},{4,8},{8,12},{1,5},{5,9},{9,13},{2,6},{6,10},{10,14},{3,7},{... | collective-permute-start | bytes 196616 | tf_op jit(solution)/shard_map/ppermute | solution.py:206
  14.2 1.3 collective-permute-start.1
  15.5 0.6 collective-permute-done
  16.1 4.3 %collective-permute-done.1 = bf16[2,8,2048]{2,1,0:T(8,128)(2,1)S(1)} collective-permute-done((bf16[2,8,2048]{2,1,0:T(8,128)(2,1)S(1)}, bf16[2,8,2048]{2,1,0:T(8,128)(2,1)S(1)}, u32[]{:S(2)}, u32[]{:S(2)}) %collective-permute-start.1) | collective-permute-done | bytes 65568 | tf_op jit(solution)/shard_map/ppermute | solution.py:207
  20.4 0.1 pad_maximum_fusion
  20.5 25.1 %all-gather.2.cloned.1.call-done.w_ref = bf16[320,2048]{1,0:T(8,128)(2,1)} async-done(((bf16[320,512]{1,0:T(8,128)(2,1)}), bf16[320,2048]{1,0:T(8,128)(2,1)}) %all-gather.2.cloned.1.call-update) | async-done | bytes 1310736 | tf_op jit(solution)/shard_map/all_gather | solution.py:208
  45.6 0.0 copy-done.1
  45.6 0.0 copy-start
  45.6 1.3 copy-done
  46.9 31.5 %shard_map.84 = (bf16[2,128,2048]{2,1,0:T(8,128)(2,1)}, bf16[2,128,2048]{2,1,0:T(8,128)(2,1)}, bf16[320,2048]{1,0:T(8,128)(2,1)}, f32[8,256]{1,0:T(8,128)S(1)}) custom-call(bf16[288,2048]{1,0:T(8,128)(2,1)S(1)} %bitcast.3, bf16[320,2048]{1,0:T(8,128)(2,1)S(1)} %copy-done, s32[1,2048]{1,0:T(1,128)S(1)} %bitcast.4), custom_call_target="tpu_custom_call" | custom-call | tf_op jit(solution)/shard_map/pallas_call | solution.py:168
  78.4 0.0 copy-start.2
  78.4 0.0 copy-start.4
  78.4 0.0 copy-start.5
  78.4 0.0 reduce-scatter.2.cloned.1.call-update
  78.4 0.0 all-reduce.2.cloned.1.call-start
  78.4 30.3 %reduce-scatter.2.cloned.1.call-done = bf16[320,512]{1,0:T(8,128)(2,1)} async-done(((bf16[320,2048]{1,0:T(8,128)(2,1)}), bf16[320,512]{1,0:T(8,128)(2,1)}) %reduce-scatter.2.cloned.1.call-update) | async-done | bytes 327696 | tf_op jit(solution)/shard_map/reduce_scatter | solution.py:213
  108.8 0.0 all-reduce.2.cloned.1.call-update
  108.8 0.6 reduce_sum.18
  109.4 31.8 %psum.21 = f32[]{:T(128)} all-reduce(f32[]{:T(128)} %reduce_sum.18), channel_id=1, replica_groups=mesh['parts'=2,'tm'=4,'dp'=4] {'tm','dp'}, use_global_device_ids=true, to_apply=%region_1.0 | all-reduce | flops 1 | bytes 8 | tf_op jit(solution)/shard_map/psum | solution.py:210
  141.2 1.1 all-reduce.2.cloned.1.call-done
  142.3 1.7 %fusion.5 = f32[]{:T(128)} fusion(bf16[320,512]{1,0:T(8,128)(2,1)} %all-reduce.2.cloned.1.call-done), kind=kLoop, calls=%fused_computation.9 | loop fusion | flops 491519 | bytes 327684 | tf_op jit(solution)/shard_map/reduce_sum | solution.py:215
  144.7 12.3 %psum.23 = f32[]{:T(128)} all-reduce(f32[]{:T(128)} %fusion.5), channel_id=1, replica_groups=mesh['parts'=2,'tm'=4,'dp'=4] {'tm'}, use_global_device_ids=true, to_apply=%region_5.0 | all-reduce | flops 1 | bytes 8 | tf_op jit(solution)/shard_map/psum | solution.py:215
  157.8 0.0 copy-done.2
  157.8 0.0 copy-done.4
  157.8 0.0 copy-done.5
  157.8 2.3 %fusion.4 = f32[320,512]{1,0:T(8,128)} fusion(bf16[320,512]{1,0:T(8,128)(2,1)} %all-reduce.2.cloned.1.call-done, f32[320,512]{1,0:T(8,128)S(1)} %copy-done.2, f32[320,512]{1,0:T(8,128)S(1)} %copy-done.4, f32[320,512]{1,0:T(8,128)S(1)} %copy-done.5, f32[]{:T(128)S(6)} %min.3), kind=kLoop, calls=%fused_computation.8 | loop fusion | flops 2457600 | bytes 2949124 | tf_op jit(solution)/shard_map/add | solution.py:198
  (1 shorter events, 0.0 us)
Async XLA Ops:
  7.2 2.1 %copy-start.3 = (bf16[2,128,2048]{2,1,0:T(8,128)(2,1)S(1)}, bf16[2,128,2048]{2,1,0:T(8,128)(2,1)}, u32[]{:S(2)}) copy-start(bf16[2,128,2048]{2,1,0:T(8,128)(2,1)} %param.5) | copy-start | bytes 3145732
  7.2 38.4 %all-gather.2.cloned.1.call-start = ((), (), s32[]{:S(2)}) async-start(), calls=%async_computation.1 | async-start | bytes 1638400 | tf_op jit(solution)/shard_map/all_gather | solution.py:208
  9.2 36.4 %copy-start.1 = (s32[2048]{0:T(1024)S(1)}, s32[2048]{0:T(1024)}, u32[]{:S(2)}) copy-start(s32[2048]{0:T(1024)} %param.9) | copy-start | bytes 24580
  9.2 99.6 %reduce-scatter.2.cloned.1.call-start = ((), (), s32[]{:S(2)}) async-start(), calls=%async_computation.2 | async-start | bytes 1638400 | tf_op jit(solution)/shard_map/reduce_scatter | solution.py:213
  9.3 6.8 %collective-permute-start = (bf16[2,8,2048]{2,1,0:T(8,128)(2,1)S(1)}, bf16[2,8,2048]{2,1,0:T(8,128)(2,1)S(1)}, u32[]{:S(2)}, u32[]{:S(2)}) collective-permute-start(bf16[2,8,2048]{2,1,0:T(8,128)(2,1)S(1)} %get-tuple-element.12), channel_id=1, source_target_pairs={{0,4},{4,8},{8,12},{1,5},{5,9},{9,13},{2,6},{6,10},{10,14},{3,7},{... | collective-permute-start | bytes 196616 | tf_op jit(solution)/shard_map/ppermute | solution.py:206
  14.2 6.2 %collective-permute-start.1 = (bf16[2,8,2048]{2,1,0:T(8,128)(2,1)S(1)}, bf16[2,8,2048]{2,1,0:T(8,128)(2,1)S(1)}, u32[]{:S(2)}, u32[]{:S(2)}) collective-permute-start(bf16[2,8,2048]{2,1,0:T(8,128)(2,1)S(1)} %get-tuple-element.13), channel_id=1, source_target_pairs={{4,0},{8,4},{12,8},{5,1},{9,5},{13,9},{6,2},{10,6},{14,10},{7,3},{... | collective-permute-start | bytes 196616 | tf_op jit(solution)/shard_map/ppermute | solution.py:207
  45.6 1.3 copy-start
  78.4 79.4 %copy-start.2 = (f32[320,512]{1,0:T(8,128)S(1)}, f32[320,512]{1,0:T(8,128)}, u32[]{:S(2)}) copy-start(f32[320,512]{1,0:T(8,128)} %param.6) | copy-start | bytes 1966084
  78.4 79.4 %copy-start.4 = (f32[320,512]{1,0:T(8,128)S(1)}, f32[320,512]{1,0:T(8,128)}, u32[]{:S(2)}) copy-start(f32[320,512]{1,0:T(8,128)} %param.8) | copy-start | bytes 1966084
  78.4 79.4 %copy-start.5 = (f32[320,512]{1,0:T(8,128)S(1)}, f32[320,512]{1,0:T(8,128)}, u32[]{:S(2)}) copy-start(f32[320,512]{1,0:T(8,128)} %param.7) | copy-start | bytes 1966084
  78.4 63.9 %all-reduce.2.cloned.1.call-start = ((), (), s32[]{:S(2)}) async-start(), calls=%async_computation.3 | async-start | bytes 655360 | tf_op jit(solution)/shard_map/psum | solution.py:214
Sparse Core Ops, SparseCore 0:
  10.2 35.3 all-gather.1
  78.5 30.1 reduce-scatter.1
  111.1 31.1 all-reduce.1

commit v2 on v1

--- a/solution.py
+++ b/solution.py
@@ -21,6 +21,7 @@
 rms_eps = 1e-06
 step_count = 100
 
+MESH = pl.DeviceIdType.MESH
 TN = (((0,), (0,)), ((), ()))
 NT = (((1,), (1,)), ((), ()))
 
@@ -76,7 +77,7 @@
     def encode(index, carry):
         cols = pl.ds(pl.multiple_of(index * WIDE, WIDE), WIDE)
         for k in range(KERNEL):
-            taps = w_ref[k * GW : (k + 1) * GW, cols].astype(jnp.float32)
+            taps = w_ref[index, k * GW : (k + 1) * GW, :].astype(jnp.float32)
             tiled = jnp.concatenate([taps] * (WIDE // GW), axis=0)
             table[index, k * WIDE : (k + 1) * WIDE, :] = jnp.where(block_mask, tiled, 0.0).astype(
                 jnp.bfloat16
@@ -153,7 +154,7 @@
         for k in range(KERNEL):
             taken = slice(k * GW, (k + 1) * GW)
             total = partial[taken, cols] + diagonal(product[:, k * WIDE : (k + 1) * WIDE])
-            grad_ref[taken, cols] = total.astype(grad_ref.dtype)
+            grad_ref[index, taken, :] = total.astype(grad_ref.dtype)
         return carry
 
     lax.fori_loop(0, blocks, finish, 0)
@@ -170,7 +171,7 @@
         out_shape=(
             jax.ShapeDtypeStruct(signal.shape, jnp.bfloat16),
             jax.ShapeDtypeStruct(signal.shape, jnp.bfloat16),
-            jax.ShapeDtypeStruct((KERNEL * GW, channels), jnp.bfloat16),
+            jax.ShapeDtypeStruct((channels // WIDE, KERNEL * GW, WIDE), jnp.bfloat16),
             jax.ShapeDtypeStruct((8, WIDE), jnp.float32),
         ),
         in_specs=[vmem] * 3,
@@ -187,6 +188,320 @@
     )(wide.reshape(rows, channels), weight, shuffle.reshape(1, channels))
 
 
+def flip(index, bit):
+    return index + bit - 2 * bit * ((index // bit) % 2)
+
+
+def bits_of(count):
+    return [1 << b for b in range(count.bit_length() - 1)]
+
+
+def greet(peers, size, members, bits, mine):
+    barrier = pltpu.get_barrier_semaphore()
+    for j in range(1, size):
+        pl.semaphore_signal(
+            barrier, inc=1, device_id={"tm": lax.rem(peers + j, size)}, device_id_type=MESH
+        )
+    for bit in bits:
+        pl.semaphore_signal(
+            barrier, inc=1, device_id={"dp": flip(mine, bit)}, device_id_type=MESH
+        )
+    pl.semaphore_wait(barrier, size - 1 + len(bits))
+
+
+def remote(src, dst, send, recv, target):
+    return pltpu.make_async_remote_copy(
+        src_ref=src, dst_ref=dst, send_sem=send, recv_sem=recv, device_id=target,
+        device_id_type=MESH,
+    )
+
+
+def gather_kernel(
+    size, members, shard_ref, first_ref, last_ref, full_ref, before_ref, after_ref,
+    send_tm, recv_tm, send_dp, recv_dp, send_halo, recv_halo, local_sem,
+):
+    me, mine = lax.axis_index("tm"), lax.axis_index("dp")
+    bits = bits_of(members)
+    greet(me, size, members, bits, mine)
+
+    to_after = remote(
+        last_ref, before_ref, send_halo.at[0], recv_halo.at[0], {"tm": jnp.minimum(me + 1, size - 1)}
+    )
+    to_before = remote(
+        first_ref, after_ref, send_halo.at[1], recv_halo.at[1], {"tm": jnp.maximum(me - 1, 0)}
+    )
+
+    @pl.when(me < size - 1)
+    def _():
+        to_after.start()
+
+    @pl.when(me > 0)
+    def _():
+        to_before.start()
+
+    outgoing = []
+    for j in range(1, size):
+        copy = remote(
+            shard_ref.at[:, mine],
+            full_ref.at[me, :, mine],
+            send_tm.at[j],
+            recv_tm.at[j],
+            {"tm": lax.rem(me + j, size)},
+        )
+        copy.start()
+        outgoing.append(copy)
+    keep = pltpu.make_async_copy(shard_ref, full_ref.at[me], local_sem)
+    keep.start()
+
+    @pl.when(me == 0)
+    def _():
+        before_ref[...] = jnp.zeros_like(before_ref)
+
+    @pl.when(me == size - 1)
+    def _():
+        after_ref[...] = jnp.zeros_like(after_ref)
+
+    owned = [mine]
+    number = 0
+    for level, bit in enumerate(reversed(bits)):
+        for j in range(1, size):
+            source = lax.rem(me - j + size, size)
+            if level == 0:
+                remote(
+                    shard_ref.at[:, mine],
+                    full_ref.at[source, :, mine],
+                    send_tm.at[j],
+                    recv_tm.at[j],
+                    {"tm": source},
+                ).wait_recv()
+            else:
+                for copy in pending[j]:
+                    copy.wait_recv()
+            for place, quarter in enumerate(owned):
+                copy = remote(
+                    full_ref.at[source, :, quarter],
+                    full_ref.at[source, :, quarter],
+                    send_dp.at[number + place, j],
+                    recv_dp.at[number + place, j],
+                    {"dp": flip(mine, bit)},
+                )
+                copy.start()
+                outgoing.append(copy)
+        pending = {
+            j: [
+                remote(
+                    full_ref.at[lax.rem(me - j + size, size), :, quarter],
+                    full_ref.at[lax.rem(me - j + size, size), :, flip(quarter, bit)],
+                    send_dp.at[number + place, j],
+                    recv_dp.at[number + place, j],
+                    {"dp": flip(mine, bit)},
+                )
+                for place, quarter in enumerate(owned)
+            ]
+            for j in range(1, size)
+        }
+        number += len(owned)
+        owned = owned + [flip(quarter, bit) for quarter in owned]
+    for j in range(1, size):
+        for copy in pending[j]:
+            copy.wait_recv()
+    for copy in outgoing:
+        copy.wait_send()
+    keep.wait()
+
+    @pl.when(me < size - 1)
+    def _():
+        to_after.wait_send()
+        to_before.wait_recv()
+
+    @pl.when(me > 0)
+    def _():
+        to_before.wait_send()
+        to_after.wait_recv()
+
+
+def gather_step(shard, first, last):
+    size, members = lax.axis_size("tm"), lax.axis_size("dp")
+    vmem = pl.BlockSpec(memory_space=pltpu.VMEM)
+    dma = pltpu.SemaphoreType.DMA
+    return pl.pallas_call(
+        functools.partial(gather_kernel, size, members),
+        out_shape=(
+            jax.ShapeDtypeStruct((size,) + shard.shape, shard.dtype),
+            jax.ShapeDtypeStruct(first.shape, first.dtype),
+            jax.ShapeDtypeStruct(last.shape, last.dtype),
+        ),
+        in_specs=[vmem] * 3,
+        out_specs=(vmem,) * 3,
+        scratch_shapes=[
+            dma((size,)), dma((size,)), dma((members, size)), dma((members, size)),
+            dma((2,)), dma((2,)), dma,
+        ],
+        compiler_params=pltpu.CompilerParams(
+            collective_id=0, has_side_effects=True, vmem_limit_bytes=32 * 1024 * 1024
+        ),
+    )(shard, first, last)
+
+
+def reduce_kernel(
+    size, members, grad_ref, square_ref, owned_ref, total_ref,
+    halves, passed, crossed, kept, incoming, tiles, tile_in,
+    send_core, recv_core, send_x, recv_x, send_tm, recv_tm, send_tile, recv_tile,
+    send_gather, recv_gather, send_sum, recv_sum,
+):
+    me, mine = lax.axis_index("tm"), lax.axis_index("dp")
+    bits = bits_of(members)
+    near, far = bits
+    partner, across = flip(mine, near), flip(mine, far)
+    corner = flip(partner, far)
+    greet(me, size, members, bits, mine)
+    outgoing = []
+
+    def begin(copy):
+        copy.start()
+        outgoing.append(copy)
+        return copy
+
+    order = list(range(1, size)) + [0]
+    target = [lax.rem(me + j, size) for j in range(size)]
+    core = {}
+    for slot, quarter in ((1, corner), (0, partner)):
+        for j in order:
+            core[slot, j] = begin(
+                remote(
+                    grad_ref.at[target[j], :, quarter],
+                    halves.at[slot, target[j]],
+                    send_core.at[slot, j],
+                    recv_core.at[slot, j],
+                    {"dp": partner},
+                )
+            )
+    x = {}
+    for j in order:
+        core[1, j].wait_recv()
+        passed[target[j]] = (
+            grad_ref[target[j], :, across].astype(jnp.float32)
+            + halves[1, target[j]].astype(jnp.float32)
+        ).astype(passed.dtype)
+        x[j] = begin(
+            remote(
+                passed.at[target[j]], crossed.at[target[j]], send_x.at[j], recv_x.at[j],
+                {"dp": across},
+            )
+        )
+    for j in order:
+        core[0, j].wait_recv()
+        x[j].wait_recv()
+        value = (
+            grad_ref[target[j], :, mine].astype(jnp.float32)
+            + halves[0, target[j]].astype(jnp.float32)
+            + crossed[target[j]].astype(jnp.float32)
+        )
+        if j == 0:
+            total = value
+        else:
+            kept[j] = value.astype(kept.dtype)
+            begin(
+                remote(
+                    kept.at[j], incoming.at[j], send_tm.at[j], recv_tm.at[j], {"tm": target[j]}
+                )
+            )
+    for j in range(1, size):
+        source = lax.rem(me - j + size, size)
+        remote(
+            kept.at[j], incoming.at[j], send_tm.at[j], recv_tm.at[j], {"tm": source}
+        ).wait_recv()
+        total = total + incoming[j].astype(jnp.float32)
+    rounded = total.astype(owned_ref.dtype)
+    owned_ref[:, mine] = rounded
+
+    def share(bit, quarter, number):
+        return begin(
+            remote(
+                owned_ref.at[:, quarter], owned_ref.at[:, quarter], send_gather.at[number],
+                recv_gather.at[number], {"dp": flip(mine, bit)},
+            )
+        )
+
+    def take(bit, quarter, number):
+        remote(
+            owned_ref.at[:, flip(quarter, bit)], owned_ref.at[:, flip(quarter, bit)],
+            send_gather.at[number], recv_gather.at[number], {"dp": flip(mine, bit)},
+        ).wait_recv()
+
+    back = rounded.astype(jnp.float32)
+    powers = (back * back).reshape(-1, 8, back.shape[-1]).sum(axis=0)
+    total_ref[...] = jnp.zeros_like(total_ref)
+    width = powers.shape[-1]
+    if width % 128 == 0:
+        folded = powers[:, :128]
+        for n in range(1, width // 128):
+            folded = folded + powers[:, n * 128 : (n + 1) * 128]
+        total_ref[8:16, :] = folded
+    else:
+        total_ref[8:16, :width] = powers
+    total_ref[0:8, :] = square_ref[:, :128] + square_ref[:, 128:]
+    tile_in[me] = total_ref[...]
+    for j in range(1, size):
+        begin(
+            remote(
+                total_ref, tile_in.at[me], send_tile.at[j], recv_tile.at[j], {"tm": target[j]}
+            )
+        )
+    share(far, mine, 0)
+    share(near, mine, 1)
+    for j in range(1, size):
+        source = lax.rem(me - j + size, size)
+        remote(
+            total_ref, tile_in.at[source], send_tile.at[j], recv_tile.at[j], {"tm": source}
+        ).wait_recv()
+    tiles[0] = tile_in[...].sum(axis=0)
+    begin(remote(tiles.at[0], tiles.at[1], send_sum.at[0], recv_sum.at[0], {"dp": across}))
+    take(far, mine, 0)
+    share(near, across, 2)
+    remote(tiles.at[0], tiles.at[1], send_sum.at[0], recv_sum.at[0], {"dp": across}).wait_recv()
+    tiles[2] = tiles[0] + tiles[1]
+    begin(remote(tiles.at[2], tiles.at[3], send_sum.at[1], recv_sum.at[1], {"dp": partner}))
+    take(near, mine, 1)
+    take(near, across, 2)
+    remote(tiles.at[2], tiles.at[3], send_sum.at[1], recv_sum.at[1], {"dp": partner}).wait_recv()
+    for copy in outgoing:
+        copy.wait_send()
+    total_ref[...] = tiles[2] + tiles[3]
+
+
+def reduce_step(gradient, squares):
+    size, parts, members, rows, width = gradient.shape
+    assert members == 4
+    vmem = pl.BlockSpec(memory_space=pltpu.VMEM)
+    dma = pltpu.SemaphoreType.DMA
+    piece = (parts, rows, width)
+    kind = jnp.bfloat16
+    return pl.pallas_call(
+        functools.partial(reduce_kernel, size, members),
+        out_shape=(
+            jax.ShapeDtypeStruct((parts, members, rows, width), kind),
+            jax.ShapeDtypeStruct((16, 128), jnp.float32),
+        ),
+        in_specs=[vmem] * 2,
+        out_specs=(vmem,) * 2,
+        scratch_shapes=[
+            pltpu.VMEM((2, size) + piece, kind),
+            pltpu.VMEM((size,) + piece, kind),
+            pltpu.VMEM((size,) + piece, kind),
+            pltpu.VMEM((size,) + piece, kind),
+            pltpu.VMEM((size,) + piece, kind),
+            pltpu.VMEM((4, 16, 128), jnp.float32),
+            pltpu.VMEM((size, 16, 128), jnp.float32),
+            dma((2, size)), dma((2, size)), dma((size,)), dma((size,)), dma((size,)),
+            dma((size,)), dma((size,)), dma((size,)), dma((3,)), dma((3,)), dma((2,)), dma((2,)),
+        ],
+        compiler_params=pltpu.CompilerParams(
+            collective_id=1, has_side_effects=True, vmem_limit_bytes=48 * 1024 * 1024
+        ),
+    )(gradient, squares)
+
+
 def adam_direction(grad_part, square_total, entries, weight_part, first_part, second_part):
     rms_value = jnp.sqrt(square_total / entries + rms_eps)
     factor = jnp.minimum(1.0, 1.0 / rms_value)
@@ -200,19 +515,33 @@
 
 def on_device(signal, weight, first_moment, second_moment, shuffle):
     windows, length, channels = signal.shape
-    peers = lax.axis_size("tm")
-    up = [(i, i + 1) for i in range(peers - 1)]
-    down = [(j, i) for i, j in up]
-    before = lax.ppermute(signal[:, length - HALO :], "tm", up)
-    after = lax.ppermute(signal[:, :HALO], "tm", down)
-    full_weight = lax.all_gather(weight.astype(jnp.bfloat16), "tm", axis=1, tiled=True)
-    decoded, back_pre, gradient, squares = local_step(signal, full_weight, shuffle, before, after)
-    square_sum = lax.psum(jnp.sum(squares), ("tm", "dp"))
-    element_count = windows * lax.axis_size("dp") * length * peers * channels
-    mean_error = (square_sum / element_count).reshape(1)
-    owned = lax.psum_scatter(gradient, "tm", scatter_dimension=1, tiled=True)
-    owned = lax.psum(owned, "dp").astype(jnp.float32)
-    square_total = lax.psum(jnp.sum(owned * owned), "tm")
+    size, members = lax.axis_size("tm"), lax.axis_size("dp")
+    depth, cols = weight.shape
+    width = WIDE if cols % WIDE == 0 else cols
+    parts, blocks = cols // width, channels // WIDE
+    rows = depth // members
+    shard = weight.astype(jnp.bfloat16).reshape(members, rows, parts, width).transpose(2, 0, 1, 3)
+    first = signal[:, :HALO].reshape(windows * HALO, channels)
+    last = signal[:, length - HALO :].reshape(windows * HALO, channels)
+    full, before, after = gather_step(shard, first, last)
+    full = (
+        full.reshape(blocks, WIDE // width, depth, width)
+        .transpose(0, 2, 1, 3)
+        .reshape(blocks, depth, WIDE)
+    )
+    before = before.reshape(windows, HALO, channels)
+    after = after.reshape(windows, HALO, channels)
+    decoded, back_pre, gradient, squares = local_step(signal, full, shuffle, before, after)
+    gradient = (
+        gradient.reshape(blocks, depth, WIDE // width, width)
+        .transpose(0, 2, 1, 3)
+        .reshape(size, parts, members, rows, width)
+    )
+    owned, totals = reduce_step(gradient, squares)
+    element_count = windows * members * length * size * channels
+    mean_error = (jnp.sum(totals[:8]) / element_count).reshape(1)
+    owned = owned.transpose(1, 2, 0, 3).reshape(depth, cols).astype(jnp.float32)
+    square_total = jnp.sum(totals[8:])
     direction = adam_direction(owned, square_total, KW * CH, weight, first_moment, second_moment)
     return (decoded, mean_error, direction, back_pre)
 

time: 168 us -> 84.4 us (0.50)
  waiting for transfers between devices: 61.5 us -> 0 us
  blocking collectives: 44.1 us -> 0 us
  Pallas kernels: 31.5 us -> 75.2 us
  between operations: 16.3 us -> 3.23 us
  starting transfers between devices: 6.34 us -> 0 us
  other arithmetic: 6.7 us -> 3.25 us
    pallas_call x0 -> x2, Pallas kernels: none -> 44.6 us  [the longest x1 24.8 us: reduce_step(): pl.pallas_call(functools.partial(reduce_kernel, size, members), out_shape...]
    psum x2 -> x0, blocking collectives: 44.1 us -> none  [the longest x1 31.8 us: on_device(): square_sum = lax.psum(jnp.sum(squares), ('tm', 'dp'))]
    reduce_scatter x1 -> x0, waiting for transfers between devices: 30.3 us -> none  [on_device(): owned = lax.psum_scatter(gradient, 'tm', scatter_dimension=1, tiled=True)]
    all_gather x1 -> x0, waiting for transfers between devices: 25.1 us -> none  [on_device(): lax.all_gather(weight.astype(jnp.bfloat16), 'tm', axis=1, tiled=True)]
    ppermute x2 -> x0, starting transfers between devices: 6.22 us -> none  [the longest x1 4.93 us: on_device(): before = lax.ppermute(signal[:, length - HALO:], 'tm', up)]
    ppermute x2 -> x0, waiting for transfers between devices: 4.86 us -> none  [the longest x1 4.27 us: on_device(): after = lax.ppermute(signal[:, :HALO], 'tm', down)]
    reduce_sum x2 -> x1, other arithmetic: 2.35 us -> 0.6 us  [on_device(): square_total = jnp.sum(totals[8:])]
  transfers between devices with their start and end apart: 5 -> 0, of which waited for: 5 -> 0; matrix products, arithmetic and copies ran while one was open for 0% -> 0% of each run, Pallas kernels for 0% -> 0%
where the time goes in v2:
time: 84.4 us; the launch traced here: 84.1 us
  Pallas kernels  75.2 us (89%)
  other arithmetic  3.25 us (4%)
  between operations  3.23 us (4%)
  local copies, waits for them, and re-layouts  2.46 us (3%)
    pallas_call x1, Pallas kernels, local_step(): pl.pallas_call(functools.partial(compute_kernel, windows, length), out_sh...  30.6 us
    pallas_call x1, Pallas kernels, reduce_step(): pl.pallas_call(functools.partial(reduce_kernel, size, members), out_shape...  24.8 us
    pallas_call x1, Pallas kernels, gather_step(): pl.pallas_call(functools.partial(gather_kernel, size, members), out_shape...  19.8 us

profile of v2, /device:TPU:0, one launch (start us, length us, event | category | flops | bytes accessed | tf_op | source)
XLA Modules:
  0.0 84.1 jit_solution(7707822480069375969)
XLA Ops:
  0.6 0.9 %slice_bitcast_fusion = (bf16[16,2048]{1,0:T(8,128)(2,1)S(1)}, bf16[16,2048]{1,0:T(8,128)(2,1)S(1)}) fusion(bf16[2,128,2048]{2,1,0:T(8,128)(2,1)} %param.5), kind=kLoop, calls=%fused_computation.10 | loop fusion | bytes 262144 | tf_op jit(solution)/shard_map/reshape | solution.py:525
  1.5 0.0 copy-start.2
  1.5 1.2 %convert_element_type.8 = bf16[320,512]{1,0:T(8,128)(2,1)S(1)} convert(f32[320,512]{1,0:T(8,128)} %param.6) | non-fusion elementwise | flops 163840 | bytes 983040 | tf_op jit(solution)/shard_map/convert_element_type | solution.py:523
  2.8 0.1 reshape.36
  2.9 0.0 copy-start
  2.9 19.8 %shard_map.84 = (bf16[4,2,4,80,256]{4,3,2,1,0:T(8,128)(2,1)S(1)}, bf16[16,2048]{1,0:T(8,128)(2,1)S(1)}, bf16[16,2048]{1,0:T(8,128)(2,1)S(1)}) custom-call(bf16[2,4,80,256]{3,2,1,0:T(8,128)(2,1)S(1)} %bitcast.22, bf16[16,2048]{1,0:T(8,128)(2,1)S(1)} %get-tuple-element.25.first_ref, bf16[16,2048]{1,0:T(8,128)(2,1)S(1)} %get-tuple-element.24.last_ref), custom_call_target="tpu_custom_call" | custom-call | tf_op jit(solution)/shard_map/pallas_call | solution.py:327
  22.7 0.0 copy-done.2
  22.8 0.1 pad_maximum_fusion
  22.8 0.0 copy-done
  22.9 30.6 %shard_map.85 = (bf16[2,128,2048]{2,1,0:T(8,128)(2,1)}, bf16[2,128,2048]{2,1,0:T(8,128)(2,1)}, bf16[8,320,256]{2,1,0:T(8,128)(2,1)S(1)}, f32[8,256]{1,0:T(8,128)S(1)}) custom-call(bf16[288,2048]{1,0:T(8,128)(2,1)S(1)} %bitcast.19, bf16[8,320,256]{2,1,0:T(8,128)(2,1)S(1)} %bitcast.20, s32[1,2048]{1,0:T(1,128)S(1)} %bitcast.25), custom_call_target="tpu_custom_call" | custom-call | tf_op jit(solution)/shard_map/pallas_call | solution.py:169
  53.4 24.8 %shard_map.86 = (bf16[2,4,80,256]{3,2,1,0:T(8,128)(2,1)S(1)}, f32[16,128]{1,0:T(8,128)S(1)}) custom-call(bf16[4,2,4,80,256]{4,3,2,1,0:T(8,128)(2,1)S(1)} %bitcast.21, f32[8,256]{1,0:T(8,128)S(1)} %get-tuple-element.18.square_ref), custom_call_target="tpu_custom_call" | custom-call | tf_op jit(solution)/shard_map/pallas_call | solution.py:480
  78.2 0.6 slice_reduce_fusion
  80.2 0.1 multiply_bitcast_fusion
  80.2 0.0 copy-start.1
  80.2 0.0 copy-start.3
  80.2 0.0 copy-start.4
  80.2 0.5 copy.10
  80.8 0.5 copy-done.1
  81.3 0.2 copy-done.3
  81.5 0.2 copy-done.4
  81.7 1.3 %fusion.5 = f32[320,512]{1,0:T(8,128)} fusion(f32[320,512]{1,0:T(8,128)S(1)} %bitcast.27, f32[320,512]{1,0:T(8,128)S(1)} %copy-done.1, f32[320,512]{1,0:T(8,128)S(1)} %copy-done.3, f32[320,512]{1,0:T(8,128)S(1)} %copy-done.4), kind=kLoop, calls=%fused_computation.7 | loop fusion | flops 2129920 | bytes 3276800 | tf_op jit(solution)/shard_map/add | solution.py:513
  (2 shorter events, 0.1 us)
Async XLA Ops:
  1.5 21.2 %copy-start.2 = (bf16[2,128,2048]{2,1,0:T(8,128)(2,1)S(1)}, bf16[2,128,2048]{2,1,0:T(8,128)(2,1)}, u32[]{:S(2)}) copy-start(bf16[2,128,2048]{2,1,0:T(8,128)(2,1)} %param.5) | copy-start | bytes 3145732
  2.9 20.0 %copy-start = (s32[2048]{0:T(1024)S(1)}, s32[2048]{0:T(1024)}, u32[]{:S(2)}) copy-start(s32[2048]{0:T(1024)} %param.9) | copy-start | bytes 24580
  80.2 1.1 %copy-start.1 = (f32[320,512]{1,0:T(8,128)S(1)}, f32[320,512]{1,0:T(8,128)}, u32[]{:S(2)}) copy-start(f32[320,512]{1,0:T(8,128)} %param.6) | copy-start | bytes 1966084
  80.2 1.3 %copy-start.3 = (f32[320,512]{1,0:T(8,128)S(1)}, f32[320,512]{1,0:T(8,128)}, u32[]{:S(2)}) copy-start(f32[320,512]{1,0:T(8,128)} %param.8) | copy-start | bytes 1966084
  80.2 1.5 %copy-start.4 = (f32[320,512]{1,0:T(8,128)S(1)}, f32[320,512]{1,0:T(8,128)}, u32[]{:S(2)}) copy-start(f32[320,512]{1,0:T(8,128)} %param.7) | copy-start | bytes 1966084

commit v3 on v2

--- a/solution.py
+++ b/solution.py
@@ -502,6 +502,397 @@
     )(gradient, squares)
 
 
+def fused_kernel(
+    size, members, windows, length,
+    signal_ref, weight_ref, shuffle_ref, rec_ref, back_ref, owned_ref, total_ref,
+    onehot, table, pre, act, back, partial, wide, full, first, last, before, after,
+    grad, square, halves, passed, crossed, kept, incoming, own_total, tiles, tile_in,
+    send_halo, recv_halo, send_w, recv_w, send_f, recv_f,
+    send_core, recv_core, send_x, recv_x, send_tm, recv_tm, send_tile, recv_tile,
+    send_gather, recv_gather, send_sum, recv_sum,
+):
+    me, mine = lax.axis_index("tm"), lax.axis_index("dp")
+    bits = bits_of(members)
+    near, far = bits
+    partner, across = flip(mine, near), flip(mine, far)
+    corner = flip(partner, far)
+    channels = signal_ref.shape[2]
+    blocks = channels // WIDE
+    parts = blocks // size
+    quarter_rows = KERNEL * GW // members
+    step = length + 2 * HALO
+    rows = windows * step
+    outgoing = []
+
+    def begin(copy):
+        copy.start()
+        outgoing.append(copy)
+        return copy
+
+    for p in range(parts):
+        for d in range(members):
+            full[me, p, d] = weight_ref[
+                d * quarter_rows : (d + 1) * quarter_rows, p * WIDE : (p + 1) * WIDE
+            ].astype(full.dtype)
+    first[...] = jnp.concatenate(
+        [signal_ref[w, 0:16, :].astype(jnp.float32)[:HALO] for w in range(windows)], axis=0
+    ).astype(first.dtype)
+    last[...] = jnp.concatenate(
+        [
+            signal_ref[w, length - 16 : length, :].astype(jnp.float32)[16 - HALO :]
+            for w in range(windows)
+        ],
+        axis=0,
+    ).astype(last.dtype)
+
+    greet(me, size, members, bits, mine)
+    target = [lax.rem(me + j, size) for j in range(size)]
+    source = [lax.rem(me - j + size, size) for j in range(size)]
+    to_after = remote(
+        last, before, send_halo.at[0], recv_halo.at[0], {"tm": jnp.minimum(me + 1, size - 1)}
+    )
+    to_before = remote(
+        first, after, send_halo.at[1], recv_halo.at[1], {"tm": jnp.maximum(me - 1, 0)}
+    )
+
+    @pl.when(me < size - 1)
+    def _():
+        to_after.start()
+
+    @pl.when(me > 0)
+    def _():
+        to_before.start()
+
+    for j in range(1, size):
+        begin(
+            remote(
+                full.at[me, :, mine], full.at[me, :, mine], send_w.at[j], recv_w.at[j],
+                {"tm": target[j]},
+            )
+        )
+
+    @pl.when(me == 0)
+    def _():
+        before[...] = jnp.zeros_like(before)
+
+    @pl.when(me == size - 1)
+    def _():
+        after[...] = jnp.zeros_like(after)
+
+    square[...] = jnp.zeros_like(square)
+
+    def mark(index, carry):
+        cols = pl.ds(pl.multiple_of(index * WIDE, WIDE), WIDE)
+        row = lax.broadcasted_iota(jnp.int32, (channels, WIDE), 0)
+        onehot[:, cols] = jnp.where(row == shuffle_ref[:, cols], 1.0, 0.0).astype(jnp.bfloat16)
+        return carry
+
+    lax.fori_loop(0, blocks, mark, 0)
+
+    def weight_copy(origin, quarter, landed, level, j, where):
+        return remote(
+            full.at[origin, :, quarter], full.at[origin, :, landed], send_f.at[level, j],
+            recv_f.at[level, j], {"dp": where},
+        )
+
+    for j in range(1, size):
+        remote(
+            full.at[me, :, mine], full.at[source[j], :, mine], send_w.at[j], recv_w.at[j],
+            {"tm": source[j]},
+        ).wait_recv()
+        begin(weight_copy(source[j], mine, mine, 0, j, across))
+        begin(weight_copy(source[j], mine, mine, 1, j, partner))
+
+    @pl.when(me < size - 1)
+    def _():
+        to_after.wait_send()
+        to_before.wait_recv()
+
+    @pl.when(me > 0)
+    def _():
+        to_before.wait_send()
+        to_after.wait_recv()
+
+    place = lax.broadcasted_iota(jnp.int32, (rows, WIDE), 0)
+    inner = lax.rem(place, step)
+    low = jnp.where(me == 0, HALO, 0)
+    high = jnp.where(me == size - 1, HALO + length, step)
+    inside = jnp.logical_and(inner >= low, inner < high)
+    block_mask = (
+        lax.broadcasted_iota(jnp.int32, (WIDE, WIDE), 0) // GW
+        == lax.broadcasted_iota(jnp.int32, (WIDE, WIDE), 1) // GW
+    )
+
+    def encode_from(origin):
+        def encode(p, carry):
+            index = origin * parts + p
+            cols = pl.ds(pl.multiple_of(index * WIDE, WIDE), WIDE)
+            weights = full[origin, p].astype(jnp.float32).reshape(KERNEL * GW, WIDE)
+            for k in range(KERNEL):
+                tiled = jnp.concatenate([weights[k * GW : (k + 1) * GW]] * (WIDE // GW), axis=0)
+                table[index, k * WIDE : (k + 1) * WIDE, :] = jnp.where(
+                    block_mask, tiled, 0.0
+                ).astype(jnp.bfloat16)
+            head = before[:, cols].astype(jnp.float32)
+            tail = after[:, cols].astype(jnp.float32)
+            pieces = []
+            for w in range(windows):
+                pieces += [
+                    head[w * HALO : (w + 1) * HALO],
+                    signal_ref[w, :, cols].astype(jnp.float32),
+                    tail[w * HALO : (w + 1) * HALO],
+                ]
+            x = jnp.concatenate(pieces, axis=0)
+            wide[:, cols] = x.astype(jnp.bfloat16)
+            stack = jnp.concatenate(
+                [shifted(x, 2 - k).astype(jnp.bfloat16) for k in range(KERNEL)], axis=1
+            )
+            value = jnp.dot(stack, table[index], preferred_element_type=jnp.float32)
+            pre[:, cols] = local_part(value, windows, length)
+            active = value / (1.0 + jnp.exp(-value))
+            act[:, cols] = jnp.where(inside, active, 0.0).astype(jnp.bfloat16)
+            return carry
+
+        lax.fori_loop(0, parts, encode, 0)
+
+    encode_from(me)
+    for j in range(1, size):
+        weight_copy(source[j], mine, across, 0, j, across).wait_recv()
+        begin(weight_copy(source[j], across, across, 2, j, partner))
+    for j in range(1, size):
+        weight_copy(source[j], mine, partner, 1, j, partner).wait_recv()
+        weight_copy(source[j], across, corner, 2, j, partner).wait_recv()
+        encode_from(source[j])
+
+    def decode(index, carry):
+        cols = pl.ds(pl.multiple_of(index * WIDE, WIDE), WIDE)
+        mixed = jnp.dot(act[...], onehot[:, cols], preferred_element_type=jnp.float32)
+        decoded = jnp.zeros((rows, WIDE), jnp.float32)
+        own_mixed = []
+        for k in range(KERNEL):
+            moved = shifted(mixed, k - 2)
+            own_mixed.append(local_part(moved, windows, length).astype(jnp.bfloat16))
+            decoded += lax.dot_general(
+                moved.astype(jnp.bfloat16),
+                table[index, k * WIDE : (k + 1) * WIDE, :],
+                NT,
+                preferred_element_type=jnp.float32,
+            )
+        error = jnp.where(inside, decoded - wide[:, cols].astype(jnp.float32), 0.0)
+        own_decoded = local_part(decoded, windows, length).astype(jnp.bfloat16)
+        for w in range(windows):
+            rec_ref[w, :, cols] = own_decoded[w * length : (w + 1) * length]
+        own_error = local_part(error, windows, length)
+        square[...] += (own_error * own_error).reshape(-1, 8, WIDE).sum(axis=0)
+        stack = jnp.concatenate(
+            [shifted(error, 2 - k).astype(jnp.bfloat16) for k in range(KERNEL)], axis=1
+        )
+        value = jnp.dot(stack, table[index], preferred_element_type=jnp.float32)
+        back[:, cols] = local_part(value, windows, length).astype(jnp.bfloat16)
+        product = lax.dot_general(
+            own_error.astype(jnp.bfloat16),
+            jnp.concatenate(own_mixed, axis=1),
+            TN,
+            preferred_element_type=jnp.float32,
+        )
+        for k in range(KERNEL):
+            partial[index, k * GW : (k + 1) * GW, :] = diagonal(
+                product[:, k * WIDE : (k + 1) * WIDE]
+            )
+        return carry
+
+    lax.fori_loop(0, blocks, decode, 0)
+
+    def finish_for(owner):
+        def finish(p, carry):
+            index = owner * parts + p
+            start = pl.multiple_of(index * WIDE, WIDE)
+            cols = pl.ds(start, WIDE)
+            restored = lax.dot_general(
+                back[...], onehot[pl.ds(start, WIDE), :], NT, preferred_element_type=jnp.float32
+            )
+            value = pre[:, cols]
+            sigma = 1.0 / (1.0 + jnp.exp(-value))
+            own = (restored * (sigma * (1.0 + value * (1.0 - sigma)))).astype(jnp.bfloat16)
+            for w in range(windows):
+                back_ref[w, :, cols] = own[w * length : (w + 1) * length]
+            spread = spread_part(own.astype(jnp.float32), windows, length)
+            stack = jnp.concatenate(
+                [shifted(spread, k - 2).astype(jnp.bfloat16) for k in range(KERNEL)], axis=1
+            )
+            product = lax.dot_general(wide[:, cols], stack, TN, preferred_element_type=jnp.float32)
+            total = partial[index] + jnp.concatenate(
+                [diagonal(product[:, k * WIDE : (k + 1) * WIDE]) for k in range(KERNEL)], axis=0
+            )
+            grad[owner, p] = total.reshape(members, quarter_rows, WIDE).astype(grad.dtype)
+            return carry
+
+        lax.fori_loop(0, parts, finish, 0)
+
+    core, x = {}, {}
+
+    def send_core_chunk(j):
+        for slot, quarter in ((1, corner), (0, partner)):
+            core[slot, j] = begin(
+                remote(
+                    grad.at[target[j], :, quarter], halves.at[slot, j], send_core.at[slot, j],
+                    recv_core.at[slot, j], {"dp": partner},
+                )
+            )
+
+    def send_x_chunk(j):
+        core[1, j].wait_recv()
+        passed[j] = (
+            grad[target[j], :, across].astype(jnp.float32) + halves[1, j].astype(jnp.float32)
+        ).astype(passed.dtype)
+        x[j] = begin(
+            remote(passed.at[j], crossed.at[j], send_x.at[j], recv_x.at[j], {"dp": across})
+        )
+
+    def send_tm_chunk(j):
+        core[0, j].wait_recv()
+        x[j].wait_recv()
+        value = (
+            grad[target[j], :, mine].astype(jnp.float32)
+            + halves[0, j].astype(jnp.float32)
+            + crossed[j].astype(jnp.float32)
+        )
+        if j == 0:
+            own_total[...] = value
+        else:
+            kept[j] = value.astype(kept.dtype)
+            begin(
+                remote(
+                    kept.at[j], incoming.at[j], send_tm.at[j], recv_tm.at[j], {"tm": target[j]}
+                )
+            )
+
+    order = list(range(1, size)) + [0]
+    for n in range(size + 2):
+        if n < size:
+            finish_for(target[order[n]])
+            send_core_chunk(order[n])
+        if 1 <= n <= size:
+            send_x_chunk(order[n - 1])
+        if n >= 2:
+            send_tm_chunk(order[n - 2])
+
+    total = own_total[...]
+    for j in range(1, size):
+        remote(
+            kept.at[j], incoming.at[j], send_tm.at[j], recv_tm.at[j], {"tm": source[j]}
+        ).wait_recv()
+        total = total + incoming[j].astype(jnp.float32)
+    rounded = total.astype(owned_ref.dtype)
+    owned_ref[:, mine] = rounded
+
+    def share(bit, quarter, number):
+        return begin(
+            remote(
+                owned_ref.at[:, quarter], owned_ref.at[:, quarter], send_gather.at[number],
+                recv_gather.at[number], {"dp": flip(mine, bit)},
+            )
+        )
+
+    def take(bit, quarter, number):
+        remote(
+            owned_ref.at[:, flip(quarter, bit)], owned_ref.at[:, flip(quarter, bit)],
+            send_gather.at[number], recv_gather.at[number], {"dp": flip(mine, bit)},
+        ).wait_recv()
+
+    back = rounded.astype(jnp.float32)
+    powers = (back * back).reshape(-1, 8, back.shape[-1]).sum(axis=0)
+    total_ref[...] = jnp.zeros_like(total_ref)
+    width = powers.shape[-1]
+    if width % 128 == 0:
+        folded = powers[:, :128]
+        for n in range(1, width // 128):
+            folded = folded + powers[:, n * 128 : (n + 1) * 128]
+        total_ref[8:16, :] = folded
+    else:
+        total_ref[8:16, :width] = powers
+    total_ref[0:8, :] = square[:, :128] + square[:, 128:]
+    tile_in[me] = total_ref[...]
+    for j in range(1, size):
+        begin(
+            remote(
+                total_ref, tile_in.at[me], send_tile.at[j], recv_tile.at[j], {"tm": target[j]}
+            )
+        )
+    share(far, mine, 0)
+    share(near, mine, 1)
+    for j in range(1, size):
+        remote(
+            total_ref, tile_in.at[source[j]], send_tile.at[j], recv_tile.at[j], {"tm": source[j]}
+        ).wait_recv()
+    tiles[0] = tile_in[...].sum(axis=0)
+    begin(remote(tiles.at[0], tiles.at[1], send_sum.at[0], recv_sum.at[0], {"dp": across}))
+    take(far, mine, 0)
+    share(near, across, 2)
+    remote(tiles.at[0], tiles.at[1], send_sum.at[0], recv_sum.at[0], {"dp": across}).wait_recv()
+    tiles[2] = tiles[0] + tiles[1]
+    begin(remote(tiles.at[2], tiles.at[3], send_sum.at[1], recv_sum.at[1], {"dp": partner}))
+    take(near, mine, 1)
+    take(near, across, 2)
+    remote(tiles.at[2], tiles.at[3], send_sum.at[1], recv_sum.at[1], {"dp": partner}).wait_recv()
+    for copy in outgoing:
+        copy.wait_send()
+    total_ref[...] = tiles[2] + tiles[3]
+
+
+def fused_step(signal, weight, shuffle):
+    size, members = lax.axis_size("tm"), lax.axis_size("dp")
+    assert members == 4
+    windows, length, channels = signal.shape
+    depth, cols = weight.shape
+    parts, blocks, quarter = cols // WIDE, channels // WIDE, depth // members
+    own, rows = windows * length, windows * (length + 2 * HALO)
+    vmem = pl.BlockSpec(memory_space=pltpu.VMEM)
+    dma = pltpu.SemaphoreType.DMA
+    kind = jnp.bfloat16
+    piece = (parts, quarter, WIDE)
+    everything = (size, parts, members, quarter, WIDE)
+    edge = pltpu.VMEM((windows * HALO, channels), kind)
+    return pl.pallas_call(
+        functools.partial(fused_kernel, size, members, windows, length),
+        out_shape=(
+            jax.ShapeDtypeStruct(signal.shape, kind),
+            jax.ShapeDtypeStruct(signal.shape, kind),
+            jax.ShapeDtypeStruct((parts, members, quarter, WIDE), kind),
+            jax.ShapeDtypeStruct((16, 128), jnp.float32),
+        ),
+        in_specs=[vmem] * 3,
+        out_specs=(vmem,) * 4,
+        scratch_shapes=[
+            pltpu.VMEM((channels, channels), kind),
+            pltpu.VMEM((blocks, KERNEL * WIDE, WIDE), kind),
+            pltpu.VMEM((own, channels), jnp.float32),
+            pltpu.VMEM((rows, channels), kind),
+            pltpu.VMEM((own, channels), kind),
+            pltpu.VMEM((blocks, depth, WIDE), jnp.float32),
+            pltpu.VMEM((rows, channels), kind),
+            pltpu.VMEM(everything, kind),
+            edge, edge, edge, edge,
+            pltpu.VMEM(everything, kind),
+            pltpu.VMEM((8, WIDE), jnp.float32),
+            pltpu.VMEM((2, size) + piece, kind),
+            pltpu.VMEM((size,) + piece, kind),
+            pltpu.VMEM((size,) + piece, kind),
+            pltpu.VMEM((size,) + piece, kind),
+            pltpu.VMEM((size,) + piece, kind),
+            pltpu.VMEM(piece, jnp.float32),
+            pltpu.VMEM((4, 16, 128), jnp.float32),
+            pltpu.VMEM((size, 16, 128), jnp.float32),
+            dma((2,)), dma((2,)), dma((size,)), dma((size,)), dma((3, size)), dma((3, size)),
+            dma((2, size)), dma((2, size)), dma((size,)), dma((size,)), dma((size,)),
+            dma((size,)), dma((size,)), dma((size,)), dma((3,)), dma((3,)), dma((2,)), dma((2,)),
+        ],
+        compiler_params=pltpu.CompilerParams(
+            collective_id=2, has_side_effects=True, vmem_limit_bytes=56 * 1024 * 1024
+        ),
+    )(signal, weight, shuffle.reshape(1, channels))
+
+
 def adam_direction(grad_part, square_total, entries, weight_part, first_part, second_part):
     rms_value = jnp.sqrt(square_total / entries + rms_eps)
     factor = jnp.minimum(1.0, 1.0 / rms_value)
@@ -520,24 +911,27 @@
     width = WIDE if cols % WIDE == 0 else cols
     parts, blocks = cols // width, channels // WIDE
     rows = depth // members
-    shard = weight.astype(jnp.bfloat16).reshape(members, rows, parts, width).transpose(2, 0, 1, 3)
-    first = signal[:, :HALO].reshape(windows * HALO, channels)
-    last = signal[:, length - HALO :].reshape(windows * HALO, channels)
-    full, before, after = gather_step(shard, first, last)
-    full = (
-        full.reshape(blocks, WIDE // width, depth, width)
-        .transpose(0, 2, 1, 3)
-        .reshape(blocks, depth, WIDE)
-    )
-    before = before.reshape(windows, HALO, channels)
-    after = after.reshape(windows, HALO, channels)
-    decoded, back_pre, gradient, squares = local_step(signal, full, shuffle, before, after)
-    gradient = (
-        gradient.reshape(blocks, depth, WIDE // width, width)
-        .transpose(0, 2, 1, 3)
-        .reshape(size, parts, members, rows, width)
-    )
-    owned, totals = reduce_step(gradient, squares)
+    if cols % WIDE == 0:
+        decoded, back_pre, owned, totals = fused_step(signal, weight, shuffle)
+    else:
+        shard = weight.astype(jnp.bfloat16).reshape(members, rows, parts, width).transpose(2, 0, 1, 3)
+        first = signal[:, :HALO].reshape(windows * HALO, channels)
+        last = signal[:, length - HALO :].reshape(windows * HALO, channels)
+        full, before, after = gather_step(shard, first, last)
+        full = (
+            full.reshape(blocks, WIDE // width, depth, width)
+            .transpose(0, 2, 1, 3)
+            .reshape(blocks, depth, WIDE)
+        )
+        before = before.reshape(windows, HALO, channels)
+        after = after.reshape(windows, HALO, channels)
+        decoded, back_pre, gradient, squares = local_step(signal, full, shuffle, before, after)
+        gradient = (
+            gradient.reshape(blocks, depth, WIDE // width, width)
+            .transpose(0, 2, 1, 3)
+            .reshape(size, parts, members, rows, width)
+        )
+        owned, totals = reduce_step(gradient, squares)
     element_count = windows * members * length * size * channels
     mean_error = (jnp.sum(totals[:8]) / element_count).reshape(1)
     owned = owned.transpose(1, 2, 0, 3).reshape(depth, cols).astype(jnp.float32)

time: 84.4 us -> 78.6 us (0.931)
  Pallas kernels: 75.2 us -> 67.1 us
  local copies, waits for them, and re-layouts: 2.46 us -> 4.4 us
    pallas_call x3 -> x1, Pallas kernels: 75.2 us -> 67.1 us  [fused_step(): pl.pallas_call(functools.partial(fused_kernel, size, members, windows, le...]
    unnamed x11 -> x13, local copies, waits for them, and re-layouts: 0.95 us -> 3.89 us
    convert_element_type x1 -> x0, other arithmetic: 1.22 us -> none  [on_device(): weight.astype(jnp.bfloat16).reshape(members, rows, parts, width)]
    reshape x3 -> x0, local copies, waits for them, and re-layouts: 1 us -> none  [the longest x1 0.89 us: on_device(): last = signal[:, length - HALO:].reshape(windows * HALO, channels)]
    mul x1, other arithmetic: 0.05 us -> 1.03 us  [adam_direction(): clipped = grad_part * factor]
where the time goes in v3:
time: 78.6 us; the launch traced here: 78.3 us
  Pallas kernels  67.1 us (85%)
  local copies, waits for them, and re-layouts  4.4 us (6%)
  other arithmetic  3.62 us (5%)
  between operations  3.16 us (4%)
    pallas_call x1, Pallas kernels, fused_step(): pl.pallas_call(functools.partial(fused_kernel, size, members, windows, le...  67.1 us
    unnamed x13, local copies, waits for them, and re-layouts  3.89 us

profile of v3, /device:TPU:0, one launch (start us, length us, event | category | flops | bytes accessed | tf_op | source)
XLA Modules:
  0.0 78.3 jit_solution(9752862019669168667)
XLA Ops:
  0.6 67.1 %shard_map.84 = (bf16[2,128,2048]{2,1,0:T(8,128)(2,1)}, bf16[2,128,2048]{2,1,0:T(8,128)(2,1)}, bf16[2,4,80,256]{3,2,1,0:T(8,128)(2,1)}, f32[16,128]{1,0:T(8,128)}) custom-call(bf16[2,128,2048]{2,1,0:T(8,128)(2,1)} %signal_ref.1, f32[320,512]{1,0:T(8,128)} %weight_ref.1, s32[1,2048]{1,0:T(1,128)} %bitcast.9), custom_call_target="tpu_custom_call" | custom-call | tf_op jit(solution)/shard_map/pallas_call | solution.py:856
  67.7 1.3 %slice_reduce_fusion = (f32[]{:T(128)}, f32[]{:T(128)}) fusion(f32[16,128]{1,0:T(8,128)} %get-tuple-element.9), kind=kLoop, calls=%fused_computation.8 | loop fusion | flops 2046 | bytes 8200 | tf_op jit(solution)/shard_map/reduce_sum | solution.py:938
  70.4 1.0 %multiply_bitcast_fusion = f32[4,80,2,256]{3,1,0,2:T(8,128)S(1)} fusion(bf16[2,4,80,256]{3,2,1,0:T(8,128)(2,1)} %get-tuple-element.10, f32[]{:T(128)S(6)} %min.3), kind=kLoop, calls=%fused_computation.7 | loop fusion | flops 327680 | bytes 983044 | tf_op jit(solution)/shard_map/mul | solution.py:899
  71.4 0.0 copy-start.4
  71.4 0.5 copy.9
  71.9 0.0 copy-start
  71.9 0.0 copy-start.3
  72.0 0.5 copy-done.4
  72.5 0.6 copy-done
  73.1 0.2 copy-done.3
  73.3 0.0 copy-start.2
  73.3 1.3 %fusion.5 = f32[320,512]{1,0:T(8,128)} fusion(f32[320,512]{1,0:T(8,128)S(1)} %bitcast.8, f32[320,512]{1,0:T(8,128)S(1)} %copy-done, f32[320,512]{1,0:T(8,128)S(1)} %copy-done.3, f32[320,512]{1,0:T(8,128)S(1)} %copy-done.4), kind=kLoop, calls=%fused_computation.6 | loop fusion | flops 2129920 | bytes 3276800 | tf_op jit(solution)/shard_map/add | solution.py:904
  74.6 0.0 copy-done.2
  74.6 0.0 copy-start.1
  74.6 1.0 %copy.13 = bf16[2,128,2048]{2,1,0:T(8,128)(2,1)} copy(bf16[2,128,2048]{2,1,0:T(8,128)(2,1)S(1)} %copy-done.2) | data formatting | bytes 2097152
  75.5 0.6 copy-done.1
  76.2 1.0 %copy.14 = bf16[2,128,2048]{2,1,0:T(8,128)(2,1)} copy(bf16[2,128,2048]{2,1,0:T(8,128)(2,1)S(1)} %copy-done.1) | data formatting | bytes 2097152
  (1 shorter events, 0.0 us)
Async XLA Ops:
  71.4 1.1 %copy-start.4 = (f32[320,512]{1,0:T(8,128)S(1)}, f32[320,512]{1,0:T(8,128)}, u32[]{:S(2)}) copy-start(f32[320,512]{1,0:T(8,128)} %param.7) | copy-start | bytes 1966084
  71.9 1.1 %copy-start = (f32[320,512]{1,0:T(8,128)S(1)}, f32[320,512]{1,0:T(8,128)}, u32[]{:S(2)}) copy-start(f32[320,512]{1,0:T(8,128)} %weight_ref.1) | copy-start | bytes 1966084
  71.9 1.3 %copy-start.3 = (f32[320,512]{1,0:T(8,128)S(1)}, f32[320,512]{1,0:T(8,128)}, u32[]{:S(2)}) copy-start(f32[320,512]{1,0:T(8,128)} %param.8) | copy-start | bytes 1966084
  73.3 1.3 %copy-start.2 = (bf16[2,128,2048]{2,1,0:T(8,128)(2,1)S(1)}, bf16[2,128,2048]{2,1,0:T(8,128)(2,1)}, u32[]{:S(2)}) copy-start(bf16[2,128,2048]{2,1,0:T(8,128)(2,1)} %get-tuple-element.18) | copy-start | bytes 3145732
  74.6 1.6 %copy-start.1 = (bf16[2,128,2048]{2,1,0:T(8,128)(2,1)S(1)}, bf16[2,128,2048]{2,1,0:T(8,128)(2,1)}, u32[]{:S(2)}) copy-start(bf16[2,128,2048]{2,1,0:T(8,128)(2,1)} %get-tuple-element.21) | copy-start | bytes 3145732

commit v4 on v3

--- a/solution.py
+++ b/solution.py
@@ -504,9 +504,10 @@
 
 def fused_kernel(
     size, members, windows, length,
-    signal_ref, weight_ref, shuffle_ref, rec_ref, back_ref, owned_ref, total_ref,
+    signal_ref, weight_ref, first_ref, second_ref, shuffle_ref,
+    rec_ref, mean_ref, direction_ref, back_ref,
     onehot, table, pre, act, back, partial, wide, full, first, last, before, after,
-    grad, square, halves, passed, crossed, kept, incoming, own_total, tiles, tile_in,
+    grad, square, halves, passed, crossed, kept, incoming, own_total, tiles, tile_in, owned_ref, total_ref,
     send_halo, recv_halo, send_w, recv_w, send_f, recv_f,
     send_core, recv_core, send_x, recv_x, send_tm, recv_tm, send_tile, recv_tile,
     send_gather, recv_gather, send_sum, recv_sum,
@@ -837,10 +838,21 @@
     remote(tiles.at[2], tiles.at[3], send_sum.at[1], recv_sum.at[1], {"dp": partner}).wait_recv()
     for copy in outgoing:
         copy.wait_send()
-    total_ref[...] = tiles[2] + tiles[3]
-
-
-def fused_step(signal, weight, shuffle):
+    sums = tiles[2] + tiles[3]
+    count = windows * members * length * size * channels
+    mean_ref[...] = jnp.sum(sums[:8], axis=(0, 1), keepdims=True) / count
+    square_total = jnp.sum(sums[8:], axis=(0, 1), keepdims=True)
+    for p in range(parts):
+        lanes = slice(p * WIDE, (p + 1) * WIDE)
+        for d in range(members):
+            taken = slice(d * quarter_rows, (d + 1) * quarter_rows)
+            direction_ref[taken, lanes] = adam_direction(
+                owned_ref[p, d].astype(jnp.float32), square_total, KW * CH,
+                weight_ref[taken, lanes], first_ref[taken, lanes], second_ref[taken, lanes],
+            )
+
+
+def fused_step(signal, weight, first_moment, second_moment, shuffle):
     size, members = lax.axis_size("tm"), lax.axis_size("dp")
     assert members == 4
     windows, length, channels = signal.shape
@@ -857,11 +869,11 @@
         functools.partial(fused_kernel, size, members, windows, length),
         out_shape=(
             jax.ShapeDtypeStruct(signal.shape, kind),
+            jax.ShapeDtypeStruct((1, 1), jnp.float32),
+            jax.ShapeDtypeStruct(weight.shape, jnp.float32),
             jax.ShapeDtypeStruct(signal.shape, kind),
-            jax.ShapeDtypeStruct((parts, members, quarter, WIDE), kind),
-            jax.ShapeDtypeStruct((16, 128), jnp.float32),
         ),
-        in_specs=[vmem] * 3,
+        in_specs=[vmem] * 5,
         out_specs=(vmem,) * 4,
         scratch_shapes=[
             pltpu.VMEM((channels, channels), kind),
@@ -883,6 +895,8 @@
             pltpu.VMEM(piece, jnp.float32),
             pltpu.VMEM((4, 16, 128), jnp.float32),
             pltpu.VMEM((size, 16, 128), jnp.float32),
+            pltpu.VMEM((parts, members, quarter, WIDE), kind),
+            pltpu.VMEM((16, 128), jnp.float32),
             dma((2,)), dma((2,)), dma((size,)), dma((size,)), dma((3, size)), dma((3, size)),
             dma((2, size)), dma((2, size)), dma((size,)), dma((size,)), dma((size,)),
             dma((size,)), dma((size,)), dma((size,)), dma((3,)), dma((3,)), dma((2,)), dma((2,)),
@@ -890,7 +904,7 @@
         compiler_params=pltpu.CompilerParams(
             collective_id=2, has_side_effects=True, vmem_limit_bytes=56 * 1024 * 1024
         ),
-    )(signal, weight, shuffle.reshape(1, channels))
+    )(signal, weight, first_moment, second_moment, shuffle.reshape(1, channels))
 
 
 def adam_direction(grad_part, square_total, entries, weight_part, first_part, second_part):
@@ -912,26 +926,28 @@
     parts, blocks = cols // width, channels // WIDE
     rows = depth // members
     if cols % WIDE == 0:
-        decoded, back_pre, owned, totals = fused_step(signal, weight, shuffle)
-    else:
-        shard = weight.astype(jnp.bfloat16).reshape(members, rows, parts, width).transpose(2, 0, 1, 3)
-        first = signal[:, :HALO].reshape(windows * HALO, channels)
-        last = signal[:, length - HALO :].reshape(windows * HALO, channels)
-        full, before, after = gather_step(shard, first, last)
-        full = (
-            full.reshape(blocks, WIDE // width, depth, width)
-            .transpose(0, 2, 1, 3)
-            .reshape(blocks, depth, WIDE)
-        )
-        before = before.reshape(windows, HALO, channels)
-        after = after.reshape(windows, HALO, channels)
-        decoded, back_pre, gradient, squares = local_step(signal, full, shuffle, before, after)
-        gradient = (
-            gradient.reshape(blocks, depth, WIDE // width, width)
-            .transpose(0, 2, 1, 3)
-            .reshape(size, parts, members, rows, width)
-        )
-        owned, totals = reduce_step(gradient, squares)
+        decoded, mean_error, direction, back_pre = fused_step(
+            signal, weight, first_moment, second_moment, shuffle
+        )
+        return (decoded, mean_error.reshape(1), direction, back_pre)
+    shard = weight.astype(jnp.bfloat16).reshape(members, rows, parts, width).transpose(2, 0, 1, 3)
+    first = signal[:, :HALO].reshape(windows * HALO, channels)
+    last = signal[:, length - HALO :].reshape(windows * HALO, channels)
+    full, before, after = gather_step(shard, first, last)
+    full = (
+        full.reshape(blocks, WIDE // width, depth, width)
+        .transpose(0, 2, 1, 3)
+        .reshape(blocks, depth, WIDE)
+    )
+    before = before.reshape(windows, HALO, channels)
+    after = after.reshape(windows, HALO, channels)
+    decoded, back_pre, gradient, squares = local_step(signal, full, shuffle, before, after)
+    gradient = (
+        gradient.reshape(blocks, depth, WIDE // width, width)
+        .transpose(0, 2, 1, 3)
+        .reshape(size, parts, members, rows, width)
+    )
+    owned, totals = reduce_step(gradient, squares)
     element_count = windows * members * length * size * channels
     mean_error = (jnp.sum(totals[:8]) / element_count).reshape(1)
     owned = owned.transpose(1, 2, 0, 3).reshape(depth, cols).astype(jnp.float32)

time: 78.6 us -> 74.5 us (0.948)
  other arithmetic: 3.62 us -> 0 us
    reduce_sum x1 -> x0, other arithmetic: 1.3 us -> none  [on_device(): square_total = jnp.sum(totals[8:])]
    add x1 -> x0, other arithmetic: 1.29 us -> none  [adam_direction(): first_hat / (jnp.sqrt(second_hat) + adam_eps) + decay_rate * weight_part]
    mul x1 -> x0, other arithmetic: 1.03 us -> none  [adam_direction(): clipped = grad_part * factor]
    unnamed x13 -> x7, local copies, waits for them, and re-layouts: 3.89 us -> 4.19 us
where the time goes in v4:
time: 74.5 us; the launch traced here: 74.3 us
  Pallas kernels  67.6 us (91%)
  local copies, waits for them, and re-layouts  4.19 us (6%)
  between operations  2.45 us (3%)
    pallas_call x1, Pallas kernels, fused_step(): pl.pallas_call(functools.partial(fused_kernel, size, members, windows, le...  67.6 us
    unnamed x7, local copies, waits for them, and re-layouts  4.19 us

profile of v4, /device:TPU:0, one launch (start us, length us, event | category | flops | bytes accessed | tf_op | source)
XLA Modules:
  0.0 74.3 jit_solution(8751360435811506182)
XLA Ops:
  0.6 67.6 %shard_map.84 = (bf16[2,128,2048]{2,1,0:T(8,128)(2,1)}, f32[1,1]{1,0:T(1,128)}, f32[320,512]{1,0:T(8,128)}, bf16[2,128,2048]{2,1,0:T(8,128)(2,1)}) custom-call(bf16[2,128,2048]{2,1,0:T(8,128)(2,1)} %signal_ref.1, f32[320,512]{1,0:T(8,128)} %weight_ref.1, f32[320,512]{1,0:T(8,128)} %first_ref.1, f32[320,512]{1,0:T(8,128)} %second_ref.1, s32[1,2048]{1,0:T(1,128)} %bitcast.2), custom_call_target="tpu_custom_call" | custom-call | tf_op jit(solution)/shard_map/pallas_call | solution.py:868
  68.3 0.0 copy-start.1
  68.3 2.4 %copy.13 = bf16[2,128,2048]{2,1,0:T(8,128)(2,1)} copy(bf16[2,128,2048]{2,1,0:T(8,128)(2,1)} %get-tuple-element.16) | data formatting | bytes 2097152
  70.6 0.0 copy-start
  71.3 0.0 copy-done.1
  71.3 0.8 %copy.15 = f32[320,512]{1,0:T(8,128)} copy(f32[320,512]{1,0:T(8,128)S(1)} %copy-done.1) | data formatting | bytes 1310720
  72.2 0.0 copy-done
  72.2 1.0 %copy.16 = bf16[2,128,2048]{2,1,0:T(8,128)(2,1)} copy(bf16[2,128,2048]{2,1,0:T(8,128)(2,1)S(1)} %copy-done) | data formatting | bytes 2097152
Async XLA Ops:
  68.3 3.1 %copy-start.1 = (f32[320,512]{1,0:T(8,128)S(1)}, f32[320,512]{1,0:T(8,128)}, u32[]{:S(2)}) copy-start(f32[320,512]{1,0:T(8,128)} %get-tuple-element.18) | copy-start | bytes 1966084
  70.6 1.5 %copy-start = (bf16[2,128,2048]{2,1,0:T(8,128)(2,1)S(1)}, bf16[2,128,2048]{2,1,0:T(8,128)(2,1)}, u32[]{:S(2)}) copy-start(bf16[2,128,2048]{2,1,0:T(8,128)(2,1)} %get-tuple-element.19) | copy-start | bytes 3145732

commit v5 on v4

--- a/solution.py
+++ b/solution.py
@@ -502,6 +502,17 @@
     )(gradient, squares)
 
 
+def in_pairs(count, body):
+    if count % 2:
+        lax.fori_loop(0, count, body, 0)
+        return
+
+    def both(index, carry):
+        return body(2 * index + 1, body(2 * index, carry))
+
+    lax.fori_loop(0, count // 2, both, 0)
+
+
 def fused_kernel(
     size, members, windows, length,
     signal_ref, weight_ref, first_ref, second_ref, shuffle_ref,
@@ -654,7 +665,7 @@
             act[:, cols] = jnp.where(inside, active, 0.0).astype(jnp.bfloat16)
             return carry
 
-        lax.fori_loop(0, parts, encode, 0)
+        in_pairs(parts, encode)
 
     encode_from(me)
     for j in range(1, size):
@@ -702,7 +713,7 @@
             )
         return carry
 
-    lax.fori_loop(0, blocks, decode, 0)
+    in_pairs(blocks, decode)
 
     def finish_for(owner):
         def finish(p, carry):
@@ -728,7 +739,7 @@
             grad[owner, p] = total.reshape(members, quarter_rows, WIDE).astype(grad.dtype)
             return carry
 
-        lax.fori_loop(0, parts, finish, 0)
+        in_pairs(parts, finish)
 
     core, x = {}, {}
 

time: 74.5 us -> 72 us (0.966)
  Pallas kernels: 67.6 us -> 65.1 us
    pallas_call x1, Pallas kernels: 67.6 us -> 65.1 us  [fused_step(): pl.pallas_call(functools.partial(fused_kernel, size, members, windows, le...]
where the time goes in v5:
time: 72 us; the launch traced here: 71.8 us
  Pallas kernels  65.1 us (90%)
  local copies, waits for them, and re-layouts  4.19 us (6%)
  between operations  2.46 us (3%)
    pallas_call x1, Pallas kernels, fused_step(): pl.pallas_call(functools.partial(fused_kernel, size, members, windows, le...  65.1 us
    unnamed x7, local copies, waits for them, and re-layouts  4.19 us

profile of v5, /device:TPU:0, one launch (start us, length us, event | category | flops | bytes accessed | tf_op | source)
XLA Modules:
  0.0 71.8 jit_solution(8576812853970515135)
XLA Ops:
  0.6 65.1 %shard_map.84 = (bf16[2,128,2048]{2,1,0:T(8,128)(2,1)}, f32[1,1]{1,0:T(1,128)}, f32[320,512]{1,0:T(8,128)}, bf16[2,128,2048]{2,1,0:T(8,128)(2,1)}) custom-call(bf16[2,128,2048]{2,1,0:T(8,128)(2,1)} %signal_ref.1, f32[320,512]{1,0:T(8,128)} %weight_ref.1, f32[320,512]{1,0:T(8,128)} %first_ref.1, f32[320,512]{1,0:T(8,128)} %second_ref.1, s32[1,2048]{1,0:T(1,128)} %bitcast.2), custom_call_target="tpu_custom_call" | custom-call | tf_op jit(solution)/shard_map/pallas_call | solution.py:879
  65.8 0.0 copy-start.1
  65.8 2.4 %copy.13 = bf16[2,128,2048]{2,1,0:T(8,128)(2,1)} copy(bf16[2,128,2048]{2,1,0:T(8,128)(2,1)} %get-tuple-element.16) | data formatting | bytes 2097152
  68.1 0.0 copy-start
  68.8 0.0 copy-done.1
  68.8 0.8 %copy.15 = f32[320,512]{1,0:T(8,128)} copy(f32[320,512]{1,0:T(8,128)S(1)} %copy-done.1) | data formatting | bytes 1310720
  69.7 0.0 copy-done
  69.7 1.0 %copy.16 = bf16[2,128,2048]{2,1,0:T(8,128)(2,1)} copy(bf16[2,128,2048]{2,1,0:T(8,128)(2,1)S(1)} %copy-done) | data formatting | bytes 2097152
Async XLA Ops:
  65.8 3.1 %copy-start.1 = (f32[320,512]{1,0:T(8,128)S(1)}, f32[320,512]{1,0:T(8,128)}, u32[]{:S(2)}) copy-start(f32[320,512]{1,0:T(8,128)} %get-tuple-element.18) | copy-start | bytes 1966084
  68.1 1.5 %copy-start = (bf16[2,128,2048]{2,1,0:T(8,128)(2,1)S(1)}, bf16[2,128,2048]{2,1,0:T(8,128)(2,1)}, u32[]{:S(2)}) copy-start(bf16[2,128,2048]{2,1,0:T(8,128)(2,1)} %get-tuple-element.19) | copy-start | bytes 3145732
